TPU v7x, 256 devices: a whole 4x4x8 slice. The times are simulated.
256 devices in a mesh: particle: 16 (over x, y_lo, core), shard: 16 (over z, y_hi).
Axes of the slice: x: 4, y: 4 (y_hi: 2, y_lo: 2; y = y_hi * 2 + y_lo), z: 8, core: 2. Of those that a mesh axis runs over, the one named last changes fastest.
Arguments:
- pool: bfloat16 [16384, 1024], P('shard'), may hold values from -6 to 6
- batch_index: int32 [8192], P('shard'), may hold values from 0 to 1023
- kernel_scale: int32 [1], replicated, may hold values from 4194304 to 8388607
- cotangent: bfloat16 [16, 8192, 1024], P('particle', 'shard'), may hold values from -6 to 6
- weights: float32 [16, 1024, 2, 2048], P('particle', 'shard'), may hold values from -10 to 10
- first_moment: float32 [16, 1024, 2, 2048], P('particle', 'shard'), may hold values from -2 to 2
- second_moment: float32 [16, 1024, 2, 2048], P('particle', 'shard'), may hold values from 0.01 to 1
Outputs:
- new_weights: float32 [16, 1024, 2, 2048], P('particle', 'shard')
- new_first: float32 [16, 1024, 2, 2048], P('particle', 'shard')
- new_second: float32 [16, 1024, 2, 2048], P('particle', 'shard')
- transport: float32 [16, 1024, 2, 2048], P('particle', 'shard')
Inputs may be any that keep to these rules, and one draw needn't show every extreme that they name: `batch_index`: each entry names a row of the pool block that the same index of shard holds.
All inputs are finite; a program needn't handle non-finite values.
Results may differ from a plain program's by a relative error of at most 0.015.
Values may be sent and summed in bfloat16 or wider, within the bound.
A program may use at most 192 MiB of HBM per device.

v0:
```python
import jax
import jax.numpy as jnp
from jax import lax
from jax.sharding import PartitionSpec as P


def gelu_pair(up_proj):
    cdf_part = 0.5 * (1.0 + jax.scipy.special.erf(up_proj * 0.7071067811865476))
    density = jnp.exp(-0.5 * up_proj * up_proj) * 0.3989422804014327
    return (up_proj * cdf_part, cdf_part + up_proj * density)


def local(pool, batch_index, kernel_scale, cotangent, weights, first_moment, second_moment):
    shard_count = lax.axis_size("shard")
    particles = lax.axis_size("particle")
    tok_rows = batch_index.shape[0]
    model_width = pool.shape[1]
    hidden_units = weights.shape[3]
    picked = jnp.take(pool, batch_index, axis=0).astype(jnp.float32)
    normed = (picked * lax.rsqrt(jnp.mean(picked * picked, axis=1, keepdims=True) + 1e-06)).astype(
        jnp.bfloat16
    )
    upstream = cotangent[0]
    local_b = weights[0].astype(jnp.bfloat16)
    block_rows = lax.all_gather(local_b, "shard", axis=0, tiled=True)
    left_cols = normed
    right_cols = upstream
    up_part = jnp.dot(left_cols, block_rows[:, 0, :], preferred_element_type=jnp.float32)
    back_part = jnp.dot(right_cols, block_rows[:, 1, :], preferred_element_type=jnp.float32)
    up_proj = up_part * model_width ** (-0.5)
    back_proj = back_part * hidden_units ** (-0.5)
    act_full, gelu_slope = gelu_pair(up_proj)
    activation = act_full.astype(jnp.bfloat16)
    up_grad = (back_proj * gelu_slope).astype(jnp.bfloat16)
    grad_scale = 1.0 / (tok_rows * shard_count * model_width)
    contract = (((0,), (0,)), ((), ()))
    left_cols = normed
    right_cols = upstream
    g_up = lax.dot_general(left_cols, up_grad, contract, preferred_element_type=jnp.float32)
    g_down = lax.dot_general(right_cols, activation, contract, preferred_element_type=jnp.float32)
    g_up = g_up * (model_width ** (-0.5) * grad_scale)
    g_down = g_down * (hidden_units ** (-0.5) * grad_scale)
    grad_sum = lax.psum_scatter(
        jnp.stack([g_up, g_down], axis=1).astype(jnp.bfloat16),
        "shard",
        scatter_dimension=0,
        tiled=True,
    ).astype(jnp.float32)
    score_b = (-grad_sum).astype(jnp.bfloat16)
    inverse_band = 1.0 / kernel_scale[0].astype(jnp.float32)
    repulse = 2.0 * inverse_band
    own_w = lax.optimization_barrier(local_b).astype(jnp.float32)
    all_w, all_scores = (
        lax.all_gather(local_b[None], "particle", axis=0, tiled=True),
        lax.all_gather(score_b[None], "particle", axis=0, tiled=True),
    )
    all_wf = all_w.astype(jnp.float32)
    offset_sq = own_w[None] - all_wf
    partial_row = jnp.sum(offset_sq * offset_sq, axis=(1, 2, 3))
    distances = lax.psum(partial_row, "shard")
    kernel = jnp.exp(-distances * inverse_band)
    kernel_total = jnp.sum(kernel)
    pushed_field = all_scores.astype(jnp.float32) - repulse * all_wf
    term_rows = (kernel[:, None, None, None] * pushed_field).astype(jnp.bfloat16)
    weighted = jnp.sum(lax.optimization_barrier(term_rows).astype(jnp.float32), axis=0)
    params_total = 2 * model_width * hidden_units
    transport = params_total / particles * (weighted + repulse * kernel_total * own_w)
    new_first = 0.9 * first_moment[0] - 0.1 * transport
    new_second = 0.999 * second_moment[0] + 0.001 * transport * transport
    new_weights = weights[0] - 0.01 * new_first / (jnp.sqrt(new_second) + 1e-08)
    return (new_weights[None], new_first[None], new_second[None], transport[None])


def solution(mesh):
    placed = (
        P("shard", None),
        P("shard"),
        P(),
        P("particle", "shard", None),
        P("particle", "shard", None, None),
        P("particle", "shard", None, None),
        P("particle", "shard", None, None),
    )
    return jax.shard_map(
        local,
        mesh=mesh,
        in_specs=placed,
        out_specs=(
            P("particle", "shard", None, None),
            P("particle", "shard", None, None),
            P("particle", "shard", None, None),
            P("particle", "shard", None, None),
        ),
        check_vma=False,
    )
```

profile of v0, /device:TPU:1, one launch (start us, length us, event | category | flops | bytes accessed | tf_op | source)
XLA Modules:
  0.0 503.9 jit_solution(2273082299362088722)
XLA Ops:
  8.1 2.6 bitcast_convert_fusion
  10.7 0.7 compare_select_fusion
  11.4 2.1 gather_fusion
  13.5 0.4 fusion.9
  13.9 137.3 %all-gather.7.cloned.1.call-done = bf16[1024,2,2048]{2,1,0:T(2,128)(2,1)} async-done(((bf16[64,2,2048]{2,1,0:T(2,128)(2,1)}), bf16[1024,2,2048]{2,1,0:T(2,128)(2,1)}) %all-gather.7.cloned.1.call-update) | async-done | bytes 8388624 | tf_op jit(solution)/shard_map/all_gather | solution.py:25
  151.3 17.1 %fusion.27 = (bf16[1024,1,2048]{2,1,0:T(2,128)(2,1)}, bf16[1024,1,2048]{2,1,0:T(2,128)(2,1)S(1)}) fusion(bf16[1024,2,2048]{2,1,0:T(2,128)(2,1)} %all-gather.7.cloned.1.call-done), kind=kLoop, calls=%fused_computation.51 | loop fusion | bytes 16777216 | tf_op jit(solution)/shard_map/slice | solution.py:29
  168.4 3.1 fusion.5
  171.6 4.2 fusion.8
  175.7 11.7 %fusion.7 = bf16[1024,1,2048]{2,0,1:T(8,128)(2,1)} fusion(f32[512,2048]{1,0:T(8,128)} %copy-done.9, bf16[1024,1,2048]{2,1,0:T(2,128)(2,1)} %get-tuple-element.10, bf16[1,512,1024]{2,1,0:T(8,128)(2,1)S(1)} %copy-done.8, f32[512]{0:T(512)S(1)} %add_rsqrt_fusion, bf16[512,1024]{1,0:T(8,128)(2,1)S(1)} %gather_fusion, pred[512]{0:T(512)(128)(4,1)S(1)} %compare_and_fusion), kind=kOutput, calls=%fused_computation.19 | convolution fusion | flops 4313841664 | bytes 14682624 | tf_op jit(solution)/shard_map/dot_general | solution.py:39
  187.4 7.5 %pad_maximum_fusion = bf16[1024,2,2048]{2,0,1:T(8,128)(2,1)} fusion(bf16[1024,1,2048]{2,0,1:T(8,128)(2,1)} %fusion.8, bf16[1024,1,2048]{2,0,1:T(8,128)(2,1)} %fusion.7), kind=kLoop, calls=%fused_computation.9 | loop fusion | flops 4194304 | bytes 16777216 | tf_op jit(solution)/shard_map/stack | solution.py:44
  194.9 0.2 all-gather.5.cloned.1.call-start
  195.1 1.0 copy-done.2
  196.1 1.4 copy.58
  197.5 0.0 all-gather.9.cloned.1.call-start
  197.5 221.5 %reduce-scatter.2.cloned.1.call-done = bf16[64,2,2048]{2,0,1:T(8,128)(2,1)} async-done(((bf16[1024,2,2048]{2,0,1:T(8,128)(2,1)}), bf16[64,2,2048]{2,0,1:T(8,128)(2,1)}) %reduce-scatter.2.cloned.1.call-update) | async-done | bytes 524304 | tf_op jit(solution)/shard_map/reduce_scatter | solution.py:43
  419.0 1.9 negate_convert_fusion
  421.0 0.2 copy.28
  421.9 5.7 %fusion.1 = f32[16]{0:T(128)S(1)} fusion(bf16[16,64,2,2048]{3,1,2,0:T(8,128)(2,1)} %all-gather.5.cloned.1.call-done, f32[64,2,2048]{2,0,1:T(8,128)S(1)} %copy.28), kind=kLoop, calls=%fused_computation.4 | loop fusion | flops 16777200 | bytes 9437248 | tf_op jit(solution)/shard_map/reduce_sum | solution.py:59
  427.6 31.4 %psum.7 = f32[16]{0:T(128)S(1)} all-reduce(f32[16]{0:T(128)S(1)} %fusion.1), channel_id=1, replica_groups=mesh['particle'=16,'shard'=16] {'shard'}, use_global_device_ids=true, to_apply=%region_1.2 | all-reduce | flops 16 | bytes 128 | tf_op jit(solution)/shard_map/psum | solution.py:60
  459.0 0.6 fusion.26
  460.3 19.6 %all-gather.9.cloned.1.call-done = bf16[1024,2,2048]{2,0,1:T(8,128)(2,1)} async-done(((bf16[64,2,2048]{2,0,1:T(8,128)(2,1)}), bf16[1024,2,2048]{2,0,1:T(8,128)(2,1)}) %all-gather.9.cloned.1.call-update) | async-done | bytes 8388624 | tf_op jit(solution)/shard_map/all_gather | solution.py:55
  479.9 7.9 %fusion.4 = bf16[16,64,2,2048]{3,1,2,0:T(8,128)(2,1)S(1)} fusion(bf16[16,64,2,2048]{3,1,2,0:T(8,128)(2,1)} %all-gather.5.cloned.1.call-done, f32[]{:T(128)S(6)} %mul_shard_map.3, f32[16]{0:T(128)S(1)} %get-tuple-element.9, bf16[16,64,2,2048]{3,1,0,2:T(8,128)(2,1)} %bitcast.51), kind=kLoop, calls=%fused_computation.7 | loop fusion | flops 25165824 | bytes 25165892 | tf_op jit(solution)/shard_map/convert_element_type | solution.py:64
  487.8 1.9 convert_reduce_fusion
  489.7 6.8 %fusion.25 = (f32[1,64,2,2048]{3,2,1,0:T(2,128)}, f32[1,64,2,2048]{3,2,1,0:T(2,128)}, f32[1,64,2,2048]{3,2,1,0:T(2,128)}, f32[1,64,2,2048]{3,2,1,0:T(2,128)}) fusion(f32[1,64,2,2048]{3,2,1,0:T(2,128)S(1)} %copy-done.5, bf16[64,2,2048]{2,1,0:T(2,128)(2,1)S(1)} %copy-done.4, f32[]{:T(128)S(6)} %mul.182, f32[64,2,2048]{2,0,1:T(8,128)S(1)} %convert_reduce_fusion, ...), kind=kLoop, calls=%fused_computation.49 | loop fusion | flops 3932160 | bytes 8912900 | tf_op jit(solution)/shard_map/broadcast_in_dim | solution.py:71
  (29 shorter events, 0.3 us)
Async XLA Ops:
  8.0 3.4 copy-start
  8.0 143.3 %all-gather.7.cloned.1.call-start = ((), (), s32[]{:S(2)}) async-start(), calls=%async_computation.2 | async-start | bytes 8912896 | tf_op jit(solution)/shard_map/all_gather | solution.py:25
  10.6 408.4 %reduce-scatter.2.cloned.1.call-start = ((), (), s32[]{:S(2)}) async-start(), calls=%async_computation.3 | async-start | bytes 8912896 | tf_op jit(solution)/shard_map/reduce_scatter | solution.py:43
  11.4 2.1 copy-start.7
  168.4 3.1 copy-start.8
  171.6 4.2 copy-start.9
  194.9 1.2 copy-start.2
  194.9 226.1 %copy-start.3 = (bf16[64,2,2048]{2,1,0:T(2,128)(2,1)S(1)}, bf16[64,2,2048]{2,1,0:T(2,128)(2,1)}, u32[]{:S(2)}) copy-start(bf16[64,2,2048]{2,1,0:T(2,128)(2,1)} %bitcast_convert_fusion) | copy-start | bytes 1572868
  194.9 227.0 %all-gather.5.cloned.1.call-start = ((), (), s32[]{:S(2)}) async-start(), calls=%async_computation.1 | async-start | bytes 8912896 | tf_op jit(solution)/shard_map/all_gather | solution.py:54
  197.5 282.4 %all-gather.9.cloned.1.call-start = ((), (), s32[]{:S(2)}) async-start(), calls=%async_computation.4 | async-start | bytes 8912896 | tf_op jit(solution)/shard_map/all_gather | solution.py:55
  487.7 1.9 copy-start.4
  487.7 1.9 copy-start.5
  487.8 1.9 copy-start.6
  487.8 8.7 %copy-start.1 = (bf16[1024,1024]{1,0:T(8,128)(2,1)S(1)}, bf16[1024,1024]{1,0:T(8,128)(2,1)}, u32[]{:S(2)}) copy-start(bf16[1024,1024]{1,0:T(8,128)(2,1)} %param.7) | copy-start | bytes 6291460
Sparse Core Ops, SparseCore 0:
  12.0 139.2 all-gather.6
  195.0 223.9 reduce-scatter.1
Sparse Core Ops, SparseCore 1:
  197.8 60.7 all-gather.4
  421.1 58.7 all-gather.8
where the time goes:
time: 504 us
  waiting for transfers between devices  379 us (75%)
  other arithmetic  36 us (7%)
  blocking collectives  31.4 us (6%)
  local copies, waits for them, and re-layouts  21.8 us (4%)
  matrix products  18.9 us (4%)
  between operations  17 us (3%)
    reduce_scatter x1, waiting for transfers between devices, local(): lax.psum_scatter(jnp.stack([g_up, g_down], axis=1).astype(jnp.bfloat16),...  221 us
    all_gather x1, waiting for transfers between devices, local(): block_rows = lax.all_gather(local_b, 'shard', axis=0, tiled=True)  137 us
    psum x1, blocking collectives, local(): distances = lax.psum(partial_row, 'shard')  31.4 us
    all_gather x1, waiting for transfers between devices, local(): lax.all_gather(score_b[None], 'particle', axis=0, tiled=True)  19.6 us
    slice x1, local copies, waits for them, and re-layouts, local(): block_rows[:, 1, :]  17.1 us
    dot_general x1, matrix products, local(): lax.dot_general(left_cols, up_grad, contract, preferred_element_type=jnp....  11.7 us
  transfers between devices with their start and end apart: 4, of which 3 were waited for; matrix products, arithmetic and copies ran while one was open for 3% of the time, Pallas kernels for 0%

commit v1 on v0

v1 whole, which is shorter than its diff:
```python
import functools

import jax
import jax.numpy as jnp
from jax import lax
from jax.experimental import pallas as pl
from jax.experimental.pallas import tpu as pltpu
from jax.sharding import PartitionSpec as P

MESH = pl.DeviceIdType.MESH
CHUNKS = 2
LANES = 128
HIGHEST = lax.Precision.HIGHEST
F32 = jnp.float32
BF16 = jnp.bfloat16


def gelu_pair(up_proj):
    cdf_part = 0.5 * (1.0 + lax.erf(up_proj * 0.7071067811865476))
    density = jnp.exp(-0.5 * up_proj * up_proj) * 0.3989422804014327
    return (up_proj * cdf_part, cdf_part + up_proj * density)


def remote(src, dst, send_sem, recv_sem, device):
    return pltpu.make_async_remote_copy(
        src_ref=src,
        dst_ref=dst,
        send_sem=send_sem,
        recv_sem=recv_sem,
        device_id=device,
        device_id_type=MESH,
    )


def stein_kernel(
    dims,
    scale_ref, idx_ref, w_hbm, pool_hbm, cot_hbm,
    out_ref,
    wf, poolv, wbr, wba, wg, na, ca, nt, ct, act, upg, rss, rsr, sc, sa, wa, fld, tr, ta,
    d1, dmine, dpart, dpair, dring, krep,
    load_sem, ex_s, ex_r, cot_s, cot_r, cot_fs, cot_fr, nseg_s, nseg_r, nb_s, nb_r,
    wa_s, wa_r, ag_s, ag_r, rs_s, rs_r, dp_s, dp_r, dh_s, dh_r, dz_s, dz_r, sa_s, sa_r, ta_s, ta_r,
):
    NP, NZ, RB, TOK, D, FF, POOL = dims
    NXY, NX = NP // 2, NP // 4
    G = NX * 2
    NT = FF // LANES
    TC = NT // 2 // CHUNKS
    CH = TC * LANES
    SEG = TOK // G
    HT = TOK // 2
    rem = lax.rem
    p, s = lax.axis_index("particle"), lax.axis_index("shard")
    c, xy = rem(p, 2), p // 2
    x, yl = xy // 2, rem(xy, 2)
    h, z = rem(s, 2), s // 2
    zdev = (
        (p, rem(z + 1, NZ) * 2 + h),
        (p, rem(z + NZ - 1, NZ) * 2 + h),
    )
    sibling = (xy * 2 + 1 - c, s)
    across = (p, z * 2 + 1 - h)
    diagonal = (xy * 2 + 1 - c, z * 2 + 1 - h)
    role = xy * 2 + h

    load_w = pltpu.make_async_copy(w_hbm, wf, load_sem.at[0])
    load_w.start()
    load_pool = pltpu.make_async_copy(pool_hbm, poolv, load_sem.at[1])
    load_pool.start()
    barrier = pltpu.get_barrier_semaphore()

    def greet(device):
        pl.semaphore_signal(barrier, inc=1, device_id=device, device_id_type=MESH)

    greet(zdev[0])
    greet(zdev[1])
    greet(diagonal)

    @pl.loop(1, NP)
    def _(d):
        greet((rem(p + d, NP), s))

    @pl.loop(0, NXY)
    def _(o):
        greet((o * 2 + c, z * 2 + 1 - h))

    load_w.wait()
    for half in range(2):
        for k in range(CHUNKS):
            for tile in range(TC):
                for j in range(2):
                    t = (half * CHUNKS + k) * TC + tile
                    v = wf[pl.ds(2 * t + j, RB, stride=2 * NT), :].astype(BF16)
                    wbr[half, k, j, :, tile * LANES:(tile + 1) * LANES] = v
                    wba[(tile * 2 + j) * 2 + half, k * RB:(k + 1) * RB, :] = v
    pl.semaphore_wait(barrier, NP + NXY + 2)

    own_rows = pl.ds(pl.multiple_of((z * 2 + h) * RB, RB), RB)
    sub_at_dest = rem(h + c, 2)

    def exchange(k, half, device):
        return remote(
            wbr.at[half, k], wg.at[k, :, own_rows, :],
            ex_s.at[k * 2 + half], ex_r.at[k * 2 + sub_at_dest], device,
        )

    def cot_half(half):
        part = cot_hbm.at[pl.ds(half * HT, HT)]
        return remote(part, ca.at[h, pl.ds(half * HT, HT)], cot_s.at[half], cot_r.at[1],
                      (xy * 2 + half, z * 2 + 1 - h))

    cot_load = pltpu.make_async_copy(cot_hbm, ca.at[h], load_sem.at[2])
    cot_full = remote(cot_hbm, ca.at[h], cot_s.at[0], cot_r.at[0], sibling)

    @pl.when(c == h)
    def _():
        for k in range(CHUNKS):
            exchange(k, 1 - c, sibling).start()
        for k in range(CHUNKS):
            wg[k, :, own_rows, :] = wbr[c, k]
        cot_load.start()
        cot_full.start()

    @pl.when(c != h)
    def _():
        for k in range(CHUNKS):
            for half in range(2):
                exchange(k, half, (xy * 2 + half, z * 2 + 1 - h)).start()
        for half in range(2):
            cot_half(half).start()

    def exchange_wait(k, sub):
        rows = pl.ds(pl.multiple_of((z * 2 + rem(h + sub, 2)) * RB, RB), RB)
        remote(wbr.at[0, k], wg.at[k, :, rows, :], ex_s.at[0], ex_r.at[k * 2 + sub], sibling).wait_recv()

    def ag(k, j, step, sub):
        b = rem(z + NZ - step, NZ) if j == 0 else rem(z + step, NZ)
        rows = pl.ds(pl.multiple_of((b * 2 + rem(h + sub, 2)) * RB, RB), RB)
        n = ((k * 2 + j) * (NZ - 1) + step) * 2 + sub
        return remote(wg.at[k, j, rows, :], wg.at[k, j, rows, :], ag_s.at[n], ag_r.at[n], zdev[j])

    def ag_wait(k, j, step, sub):
        b = rem(z + 2 * NZ - 1 - step, NZ) if j == 0 else rem(z + 1 + step, NZ)
        rows = pl.ds(pl.multiple_of((b * 2 + rem(h + sub, 2)) * RB, RB), RB)
        n = ((k * 2 + j) * (NZ - 1) + step) * 2 + sub
        remote(wg.at[k, j, rows, :], wg.at[k, j, rows, :], ag_s.at[n], ag_r.at[n], zdev[j]).wait_recv()

    def ag_relay(k, step, last=None):
        for sub in range(2):
            for j in range(2):
                ag_wait(k, j, step, sub)
                if last is None:
                    @pl.when(step < NZ - 2)
                    def _():
                        ag(k, j, step + 1, sub).start()
                elif not last:
                    ag(k, j, step + 1, sub).start()

    for k in range(CHUNKS):
        @pl.when(c != h)
        def _():
            exchange_wait(k, 0)
        for j in range(2):
            ag(k, j, 0, 0).start()

    load_pool.wait()
    TB = min(LANES, TOK)

    @pl.loop(0, TOK // TB)
    def _(blk):
        at = pl.multiple_of(blk * TB, TB)
        col = jnp.broadcast_to(idx_ref[:, pl.ds(at, TB)], (LANES, TB)).T
        lane = lax.broadcasted_iota(jnp.int32, (TB, LANES), 1)
        onehot = jnp.concatenate(
            [jnp.where(col == lane + i * LANES, 1.0, 0.0).astype(BF16) for i in range(POOL // LANES)], axis=1
        )
        picked = jnp.dot(onehot, poolv[...], preferred_element_type=F32)
        mean = jnp.mean(picked * picked, axis=1, keepdims=True)
        na[h, pl.ds(at, TB), :] = (picked * lax.rsqrt(mean + 1e-06)).astype(BF16)

    seg = x * 2 + c
    own_seg = na.at[h, pl.ds(pl.multiple_of(seg * SEG, SEG), SEG)]
    nseg = remote(own_seg, own_seg, nseg_s, nseg_r, across)
    nseg.start()

    for k in range(CHUNKS):
        exchange_wait(k, 1)
        for j in range(2):
            ag(k, j, 0, 1).start()

    def slice_out(d):
        q = rem(p + d, NP)
        return remote(wba.at[q], wa.at[p], wa_s.at[d], wa_r.at[d], (q, s))

    def slice_wait(d):
        q = rem(p + NP - d, NP)
        remote(wba.at[q], wa.at[q], wa_s.at[d], wa_r.at[d], (q, s)).wait_recv()

    @pl.loop(1, NP)
    def _(d):
        slice_out(d).start()

    wa[p] = wba[p]

    got_seg = na.at[1 - h, pl.ds(pl.multiple_of(seg * SEG, SEG), SEG)]

    def seg_out(d):
        g = rem(seg + d, G)
        return remote(got_seg, got_seg, nb_s.at[d], nb_r.at[d], ((g // 2 * 2 + yl) * 2 + rem(g, 2), s))

    def seg_wait(d):
        g = rem(seg + G - d, G)
        part = na.at[1 - h, pl.ds(pl.multiple_of(g * SEG, SEG), SEG)]
        remote(part, part, nb_s.at[d], nb_r.at[d], sibling).wait_recv()

    def share_segments():
        remote(got_seg, got_seg, nseg_s, nseg_r, across).wait_recv()

        @pl.loop(1, G)
        def _(d):
            seg_out(d).start()

    cot_mine = ca.at[1 - h, pl.ds(pl.multiple_of(c * HT, HT), HT)]
    cot_other = ca.at[1 - h, pl.ds(pl.multiple_of((1 - c) * HT, HT), HT)]
    cot_pass = remote(cot_mine, cot_mine, cot_fs, cot_fr, sibling)

    def pass_cotangent():
        remote(cot_mine, cot_mine, cot_s.at[0], cot_r.at[1], sibling).wait_recv()
        cot_pass.start()

    eye = lax.broadcasted_iota(jnp.int32, (NP, LANES), 0) == lax.broadcasted_iota(jnp.int32, (NP, LANES), 1)

    def part_out(d):
        q = rem(p + d, NP)
        return remote(dmine, dpart.at[p], dp_s.at[d], dp_r.at[d], (q, s))

    def part_wait(d):
        q = rem(p + NP - d, NP)
        remote(dmine, dpart.at[q], dp_s.at[d], dp_r.at[d], (q, s)).wait_recv()

    def partial_distances():
        @pl.loop(1, NP)
        def _(d):
            slice_wait(d)

        @pl.loop(0, NP)
        def _(i):
            own = wa[i].astype(F32)
            for j in range(NP):
                off = own - wa[j].astype(F32)
                d1[i, j:j + 1, :] = jnp.sum(off * off, axis=0, keepdims=True)

        flat = d1[...].reshape(NP * NP, LANES)
        spread = jnp.dot(flat, jnp.ones((LANES, LANES), F32), precision=HIGHEST, preferred_element_type=F32)
        for i in range(NP):
            dmine[i:i + 1, :] = jnp.sum(
                jnp.where(eye, spread[i * NP:(i + 1) * NP, :], 0.0), axis=0, keepdims=True
            )

        @pl.loop(1, NP)
        def _(d):
            part_out(d).start()

    pair_out = remote(dpair.at[0], dpair.at[1], dh_s, dh_r, across)

    def pair_distances():
        dpart[p] = dmine[...]

        @pl.loop(1, NP)
        def _(d):
            part_wait(d)

        dpair[0] = jnp.sum(dpart[...], axis=0)
        pair_out.start()

    def ring_out(step):
        b = rem(z + NZ - step, NZ)
        return remote(dring.at[b], dring.at[b], dz_s.at[step], dz_r.at[step], zdev[0])

    def ring_wait(step):
        b = rem(z + 2 * NZ - 1 - step, NZ)
        remote(dring.at[b], dring.at[b], dz_s.at[step], dz_r.at[step], zdev[0]).wait_recv()

    def ring_start():
        pair_out.wait_recv()
        dring[z] = dpair[0] + dpair[1]
        ring_out(0).start()

    def ring_relay(step, last=None):
        ring_wait(step)
        if last is None:
            @pl.when(step < NZ - 2)
            def _():
                ring_out(step + 1).start()
        elif not last:
            ring_out(step + 1).start()

    inverse_band = 1.0 / jnp.full((1, LANES), scale_ref[0], jnp.int32).astype(F32)
    repulse = 2.0 * inverse_band

    def kernel_matrix():
        near = jnp.exp(-jnp.sum(dring[...], axis=0) * inverse_band)
        for i in range(NP):
            d1[i] = jnp.where(eye, jnp.broadcast_to(near[i:i + 1, :], (NP, LANES)), 0.0)
        flat = d1[...].reshape(NP * NP, LANES)
        spread = jnp.dot(flat, jnp.ones((LANES, LANES), F32), precision=HIGHEST, preferred_element_type=F32)
        krep[...] = spread.reshape(NP, NP, LANES)

    def hidden(k, blk, flip):
        hb = rem(h + blk // 2, 2)
        at = pl.multiple_of(rem(blk, 2) * HT, HT)
        normed = na[hb, pl.ds(at, HT), :]
        upstream = ca[hb, pl.ds(at, HT), :]
        rows = pl.multiple_of(hb * TOK + at, HT)
        up_proj = jnp.dot(normed, wg[k, 0], preferred_element_type=F32) * D ** (-0.5)
        back_proj = jnp.dot(upstream, wg[k, 1], preferred_element_type=F32) * FF ** (-0.5)
        act_full, gelu_slope = gelu_pair(up_proj)
        act[k, pl.ds(rows, HT), :] = act_full.astype(BF16)
        upg[k, pl.ds(rows, HT), :] = (back_proj * gelu_slope).astype(BF16)
        if flip:
            nt[:, pl.ds(rows, HT)] = normed.T
            ct[:, pl.ds(rows, HT)] = upstream.T

    def gradient(k, j, b):
        lhs = (nt if j == 0 else ct)[pl.ds(pl.multiple_of(b * 2 * RB, 2 * RB), 2 * RB), :]
        return jnp.dot(lhs, (upg if j == 0 else act)[k], preferred_element_type=F32)

    def rs(k, j, step, sub):
        n = ((k * 2 + j) * (NZ - 1) + step) * 2 + sub
        return remote(rss.at[n], rsr.at[n], rs_s.at[n], rs_r.at[n], zdev[j])

    def rs_step(k, step, first=False):
        parts = [
            gradient(k, 0, rem(z + 2 * NZ - 1 - step, NZ)),
            gradient(k, 1, rem(z + 1 + step, NZ)),
        ]
        for sub in range(2):
            for j in range(2):
                total = parts[j][sub * RB:(sub + 1) * RB, :]
                n = ((k * 2 + j) * (NZ - 1) + step) * 2 + sub
                if not first:
                    rs(k, j, step - 1, sub).wait_recv()
                    total = total + rsr[n - 2].astype(F32)
                rss[n] = total.astype(BF16)
                rs(k, j, step, sub).start()

    grad_scale = 1.0 / (TOK * NZ * 2 * D)

    def rs_final(k):
        for j in range(2):
            part = gradient(k, j, z)
            factor = (D if j == 0 else FF) ** (-0.5) * grad_scale
            for sub in range(2):
                n = ((k * 2 + j) * (NZ - 1) + NZ - 2) * 2 + sub
                rs(k, j, NZ - 2, sub).wait_recv()
                total = part[sub * RB:(sub + 1) * RB, :] + rsr[n].astype(F32)
                score = (total * -factor).astype(BF16)
                for tile in range(TC):
                    sc[k, sub, tile * 2 + j] = score[:, tile * LANES:(tile + 1) * LANES]

    def score_out(k, d):
        r = rem(role + d, NP)
        return remote(sc.at[k, rem(r, 2), r // 2], sa.at[k, role], sa_s.at[k * NP + d], sa_r.at[k * NP + d],
                      (r // 2 * 2 + c, z * 2 + rem(r, 2)))

    def score_wait(k, d):
        r = rem(role + NP - d, NP)
        remote(sc.at[k, 0, 0], sa.at[k, r], sa_s.at[k * NP + d], sa_r.at[k * NP + d], sibling).wait_recv()

    def send_scores(k):
        @pl.loop(1, NP)
        def _(d):
            score_out(k, d).start()

        sa[k, role] = sc[k, h, xy]

    def transport_out(k, d):
        q = rem(p + d, NP)
        return remote(tr.at[k, q], ta.at[k, p], ta_s.at[k * NP + d], ta_r.at[k * NP + d], (q, s))

    def transport_wait(k, d):
        q = rem(p + NP - d, NP)
        remote(tr.at[k, 0], ta.at[k, q], ta_s.at[k * NP + d], ta_r.at[k * NP + d], sibling).wait_recv()

    params_total = 2 * D * FF

    def move(k):
        @pl.loop(1, NP)
        def _(d):
            score_wait(k, d)

        for q in range(NP):
            fld[q] = sa[k, q].astype(F32) - repulse * wa[q, k * RB:(k + 1) * RB, :].astype(F32)

        @pl.loop(0, NP)
        def _(i):
            weighted = krep[i, 0:1, :] * fld[0]
            for j in range(1, NP):
                weighted = weighted + krep[i, j:j + 1, :] * fld[j]
            kernel_total = jnp.sum(krep[i], axis=0, keepdims=True)
            own_w = wa[i, k * RB:(k + 1) * RB, :].astype(F32)
            tr[k, i] = (params_total / NP * (weighted + repulse * kernel_total * own_w)).astype(BF16)

        @pl.loop(1, NP)
        def _(d):
            transport_out(k, d).start()

        ta[k, p] = tr[k, p]

    def collect(k):
        @pl.loop(1, NP)
        def _(d):
            transport_wait(k, d)

        for q in range(NP):
            o, half = q // 2, q % 2
            t = (half * CHUNKS + k) * TC + o // 2
            out_ref[pl.ds(2 * t + o % 2, RB, stride=2 * NT), :] = ta[k, q].astype(F32)

    LAST = NZ - 2
    for step in range(NZ - 1):
        ag_relay(0, step, step == LAST)
        if step == min(3, LAST):
            share_segments()
        if step == min(4, LAST):
            partial_distances()
    pair_distances()
    pass_cotangent()

    @pl.when(c == h)
    def _():
        cot_load.wait()

    @pl.when(c != h)
    def _():
        remote(cot_hbm, ca.at[h], cot_s.at[0], cot_r.at[0], sibling).wait_recv()

    ring_start()
    EARLY = min(4, NZ - 1)

    @pl.loop(0, 4)
    def _(blk):
        @pl.when(blk == 2)
        def _():
            @pl.loop(1, G)
            def _(d):
                seg_wait(d)

            remote(cot_other, cot_other, cot_fs, cot_fr, sibling).wait_recv()

        hidden(0, blk, True)

        @pl.when(blk < EARLY)
        def _():
            ag_relay(1, blk)
            ring_relay(blk)

    rs_step(0, 0, True)
    for step in range(EARLY, NZ - 1):
        ag_relay(1, step, step == LAST)
        ring_relay(step, step == LAST)
        rs_step(0, step - EARLY + 1)
    kernel_matrix()
    DONE = NZ - 1 - EARLY

    @pl.loop(0, 4)
    def _(blk):
        hidden(1, blk, False)

        @pl.when(DONE + 1 + blk <= LAST)
        def _():
            rs_step(0, DONE + 1 + blk)

    rs_step(1, 0, True)
    rs_final(0)
    send_scores(0)
    for step in range(1, NZ - 1):
        rs_step(1, step)
        if step == min(3, LAST):
            move(0)
        if step == min(6, LAST):
            collect(0)
    rs_final(1)
    send_scores(1)
    move(1)
    collect(1)

    @pl.when(c == h)
    def _():
        for k in range(CHUNKS):
            exchange(k, 1 - c, sibling).wait_send()
        cot_full.wait_send()

    @pl.when(c != h)
    def _():
        for k in range(CHUNKS):
            for half in range(2):
                exchange(k, half, (xy * 2 + half, z * 2 + 1 - h)).wait_send()
        for half in range(2):
            cot_half(half).wait_send()

    nseg.wait_send()
    cot_pass.wait_send()
    pair_out.wait_send()

    @pl.loop(1, G)
    def _(d):
        seg_out(d).wait_send()

    @pl.loop(1, NP)
    def _(d):
        slice_out(d).wait_send()
        part_out(d).wait_send()
        for k in range(CHUNKS):
            score_out(k, d).wait_send()
            transport_out(k, d).wait_send()

    @pl.loop(0, NZ - 1)
    def _(step):
        ring_out(step).wait_send()
        for k in range(CHUNKS):
            for j in range(2):
                for sub in range(2):
                    ag(k, j, step, sub).wait_send()
                    rs(k, j, step, sub).wait_send()


def stein_transport(NP, NS, kernel_scale, batch_index, flat_w, pool, cotangent):
    NZ = NS // 2
    TOK, D = cotangent.shape
    RB = D // NS
    FF = flat_w.shape[0] * LANES // RB // 2
    POOL = pool.shape[0]
    NXY, G = NP // 2, NP // 2
    TC = FF // LANES // 2 // CHUNKS
    CH = TC * LANES
    assert TC * 2 == NXY
    dma = pltpu.SemaphoreType.DMA
    ring = CHUNKS * 2 * (NZ - 1) * 2
    scratch = [
        pltpu.VMEM(flat_w.shape, F32),
        pltpu.VMEM((POOL, D), BF16),
        pltpu.VMEM((2, CHUNKS, 2, RB, CH), BF16),
        pltpu.VMEM((NP, CHUNKS * RB, LANES), BF16),
        pltpu.VMEM((CHUNKS, 2, D, CH), BF16),
        pltpu.VMEM((2, TOK, D), BF16),
        pltpu.VMEM((2, TOK, D), BF16),
        pltpu.VMEM((D, 2 * TOK), BF16),
        pltpu.VMEM((D, 2 * TOK), BF16),
        pltpu.VMEM((CHUNKS, 2 * TOK, CH), BF16),
        pltpu.VMEM((CHUNKS, 2 * TOK, CH), BF16),
        pltpu.VMEM((ring, RB, CH), BF16),
        pltpu.VMEM((ring, RB, CH), BF16),
        pltpu.VMEM((CHUNKS, 2, NXY, RB, LANES), BF16),
        pltpu.VMEM((CHUNKS, NP, RB, LANES), BF16),
        pltpu.VMEM((NP, CHUNKS * RB, LANES), BF16),
        pltpu.VMEM((NP, RB, LANES), F32),
        pltpu.VMEM((CHUNKS, NP, RB, LANES), BF16),
        pltpu.VMEM((CHUNKS, NP, RB, LANES), BF16),
        pltpu.VMEM((NP, NP, LANES), F32),
        pltpu.VMEM((NP, LANES), F32),
        pltpu.VMEM((NP, NP, LANES), F32),
        pltpu.VMEM((2, NP, LANES), F32),
        pltpu.VMEM((NZ, NP, LANES), F32),
        pltpu.VMEM((NP, NP, LANES), F32),
        dma((3,)),
        dma((2 * CHUNKS,)), dma((2 * CHUNKS,)),
        dma((2,)), dma((2,)), dma(()), dma(()),
        dma(()), dma(()), dma((G,)), dma((G,)),
        dma((NP,)), dma((NP,)),
        dma((ring,)), dma((ring,)), dma((ring,)), dma((ring,)),
        dma((NP,)), dma((NP,)), dma(()), dma(()),
        dma((NZ - 1,)), dma((NZ - 1,)),
        dma((CHUNKS * NP,)), dma((CHUNKS * NP,)), dma((CHUNKS * NP,)), dma((CHUNKS * NP,)),
    ]
    anywhere = pl.BlockSpec(memory_space=pl.ANY)
    vmem = pl.BlockSpec(memory_space=pltpu.VMEM)
    return pl.pallas_call(
        functools.partial(stein_kernel, (NP, NZ, RB, TOK, D, FF, POOL)),
        out_shape=jax.ShapeDtypeStruct(flat_w.shape, F32),
        in_specs=[pl.BlockSpec(memory_space=pltpu.SMEM), vmem, anywhere, anywhere, anywhere],
        out_specs=vmem,
        scratch_shapes=scratch,
        compiler_params=pltpu.CompilerParams(
            collective_id=0, has_side_effects=True, vmem_limit_bytes=60 * 1024 * 1024
        ),
        name="stein",
    )(kernel_scale, batch_index.reshape(1, TOK), flat_w, pool, cotangent)


def local(NP, NS, pool, batch_index, kernel_scale, cotangent, weights, first_moment, second_moment):
    rows, pair, hidden_units = weights.shape[1:]

    def flatten(a):
        return a.reshape(rows, pair, hidden_units // LANES, LANES).transpose(0, 2, 1, 3).reshape(-1, LANES)

    def unflatten(a):
        a = a.reshape(rows, hidden_units // LANES, pair, LANES).transpose(0, 2, 1, 3)
        return a.reshape(1, rows, pair, hidden_units)

    flat_w = flatten(weights[0])
    transport = stein_transport(NP, NS, kernel_scale, batch_index, flat_w, pool, cotangent[0])
    new_first = 0.9 * flatten(first_moment[0]) - 0.1 * transport
    new_second = 0.999 * flatten(second_moment[0]) + 0.001 * transport * transport
    new_weights = flat_w - 0.01 * new_first / (jnp.sqrt(new_second) + 1e-08)
    return tuple(unflatten(a) for a in (new_weights, new_first, new_second, transport))


def solution(mesh):
    placed = (
        P("shard", None),
        P("shard"),
        P(),
        P("particle", "shard", None),
        P("particle", "shard", None, None),
        P("particle", "shard", None, None),
        P("particle", "shard", None, None),
    )
    return jax.shard_map(
        functools.partial(local, mesh.shape["particle"], mesh.shape["shard"]),
        mesh=mesh,
        in_specs=placed,
        out_specs=(P("particle", "shard", None, None),) * 4,
        check_vma=False,
    )
```

time: 504 us -> 152 us (0.30)
  waiting for transfers between devices: 379 us -> 0 us
  Pallas kernels: 0 us -> 145 us
  other arithmetic: 36 us -> 3.1 us
  blocking collectives: 31.4 us -> 0 us
  local copies, waits for them, and re-layouts: 21.8 us -> 1.6 us
  matrix products: 18.9 us -> 0 us
  between operations: 17 us -> 1.35 us
    reduce_scatter x1 -> x0, waiting for transfers between devices: 221 us -> none  [local(): lax.psum_scatter(jnp.stack([g_up, g_down], axis=1).astype(jnp.bfloat16),...]
    all_gather x3 -> x0, waiting for transfers between devices: 157 us -> none  [the longest x1 137 us: local(): block_rows = lax.all_gather(local_b, 'shard', axis=0, tiled=True)]
    pallas_call x0 -> x1, Pallas kernels: none -> 145 us  [stein_transport(): pl.pallas_call(functools.partial(stein_kernel, (NP, NZ, RB, TOK, D, FF, P...]
    psum x1 -> x0, blocking collectives: 31.4 us -> none  [local(): distances = lax.psum(partial_row, 'shard')]
    dot_general x3 -> x0, matrix products: 18.9 us -> none  [the longest x1 11.7 us: local(): lax.dot_general(left_cols, up_grad, contract, preferred_element_type=jnp....]
    slice x1 -> x0, local copies, waits for them, and re-layouts: 17.1 us -> none  [local(): block_rows[:, 1, :]]
    convert_element_type x3 -> x0, other arithmetic: 12.4 us -> none  [the longest x1 7.86 us: local(): (kernel[:, None, None, None] * pushed_field).astype(jnp.bfloat16)]
    reduce_sum x4 -> x0, other arithmetic: 8.67 us -> none  [the longest x1 5.73 us: local(): partial_row = jnp.sum(offset_sq * offset_sq, axis=(1, 2, 3))]
  transfers between devices with their start and end apart: 4 -> 0, of which waited for: 3 -> 0; matrix products, arithmetic and copies ran while one was open for 3% -> 0% of each run, Pallas kernels for 0% -> 0%
where the time goes in v1:
time: 152 us; the launch traced here: 151 us
  Pallas kernels  145 us (95%)
  other arithmetic  3.1 us (2%)
  local copies, waits for them, and re-layouts  1.6 us (1%)
    pallas_call x1, Pallas kernels, stein_transport(): pl.pallas_call(functools.partial(stein_kernel, (NP, NZ, RB, TOK, D, FF, P...  145 us

profile of v1, /device:TPU:1, one launch (start us, length us, event | category | flops | bytes accessed | tf_op | source)
XLA Modules:
  0.0 151.4 jit_solution(9966761640521097930)
XLA Ops:
  1.3 0.0 copy-start.2
  1.3 145.4 %stein.1 = f32[2048,128]{1,0:T(8,128)} custom-call(s32[1]{0:T(128)S(6)} %copy.19.scale_ref, s32[1,512]{1,0:T(1,128)} %bitcast.46, f32[2048,128]{1,0:T(8,128)} %bitcast.38, bf16[1024,1024]{1,0:T(8,128)(2,1)} %pool_hbm.1, bf16[512,1024]{1,0:T(8,128)(2,1)} %bitcast.42), custom_call_target="tpu_custom_call" | custom-call | tf_op jit(solution)/shard_map/stein/pallas_call | solution.py:578
  146.7 0.0 copy-start.3
  146.7 0.0 copy-done.2
  146.7 0.0 copy-start
  146.7 0.0 copy-start.1
  146.7 0.6 broadcast_multiply_fusion.1
  147.3 0.6 copy-done.3
  147.9 0.6 broadcast_multiply_fusion
  148.5 0.0 copy-done
  148.5 0.0 copy-done.1
  148.6 1.9 %divide_subtract_fusion = (f32[2048,128]{1,0:T(8,128)}, f32[2048,128]{1,0:T(8,128)}, f32[2048,128]{1,0:T(8,128)}) fusion(f32[2048,128]{1,0:T(8,128)S(1)} %bitcast.39, f32[2048,128]{1,0:T(8,128)S(1)} %bitcast.40, f32[2048,128]{1,0:T(8,128)S(1)} %copy-done, f32[2048,128]{1,0:T(8,128)S(1)} %bitcast.41), kind=kLoop, calls=%fused_computation.2 | loop fusion | flops 2359296 | bytes 7340032 | tf_op jit(solution)/shard_map/sub | solution.py:605
  150.5 1.0 copy.20
Async XLA Ops:
  1.3 145.4 %copy-start.2 = (f32[1,64,2,2048]{3,2,1,0:T(2,128)S(1)}, f32[1,64,2,2048]{3,2,1,0:T(2,128)}, u32[]{:S(2)}) copy-start(f32[1,64,2,2048]{3,2,1,0:T(2,128)} %param.12) | copy-start | bytes 3145732
  146.7 1.2 copy-start.3
  146.7 1.8 %copy-start = (f32[2048,128]{1,0:T(8,128)S(1)}, f32[2048,128]{1,0:T(8,128)}, u32[]{:S(2)}) copy-start(f32[2048,128]{1,0:T(8,128)} %stein.1) | copy-start | bytes 3145732
  146.7 1.8 %copy-start.1 = (f32[1,64,2,2048]{3,2,1,0:T(2,128)S(1)}, f32[1,64,2,2048]{3,2,1,0:T(2,128)}, u32[]{:S(2)}) copy-start(f32[1,64,2,2048]{3,2,1,0:T(2,128)} %param.11) | copy-start | bytes 3145732

commit v2 on v1

--- a/solution.py
+++ b/solution.py
@@ -37,11 +37,12 @@
     scale_ref, idx_ref, w_hbm, pool_hbm, cot_hbm,
     out_ref,
     wf, poolv, wbr, wba, wg, na, ca, nt, ct, act, upg, rss, rsr, sc, sa, wa, fld, tr, ta,
-    d1, dmine, dpart, dpair, dring, krep,
+    d1, dmine, dpart, dpair, krep,
     load_sem, ex_s, ex_r, cot_s, cot_r, cot_fs, cot_fr, nseg_s, nseg_r, nb_s, nb_r,
-    wa_s, wa_r, ag_s, ag_r, rs_s, rs_r, dp_s, dp_r, dh_s, dh_r, dz_s, dz_r, sa_s, sa_r, ta_s, ta_r,
+    wa_s, wa_r, ag_s, ag_r, rs_s, rs_r, dp_s, dp_r, dh_s, dh_r, sa_s, sa_r, ta_s, ta_r,
 ):
-    NP, NZ, RB, TOK, D, FF, POOL = dims
+    NP, NS, RB, TOK, D, FF, POOL = dims
+    NZ = NS // 2
     NXY, NX = NP // 2, NP // 4
     G = NX * 2
     NT = FF // LANES
@@ -75,6 +76,8 @@
     greet(zdev[0])
     greet(zdev[1])
     greet(diagonal)
+    for bit in range(1, NZ.bit_length() - 1):
+        greet((p, s + (2 << bit) - (4 << bit) * rem(z // (1 << bit), 2)))
 
     @pl.loop(1, NP)
     def _(d):
@@ -93,7 +96,7 @@
                     v = wf[pl.ds(2 * t + j, RB, stride=2 * NT), :].astype(BF16)
                     wbr[half, k, j, :, tile * LANES:(tile + 1) * LANES] = v
                     wba[(tile * 2 + j) * 2 + half, k * RB:(k + 1) * RB, :] = v
-    pl.semaphore_wait(barrier, NP + NXY + 2)
+    pl.semaphore_wait(barrier, NP + NXY + NZ.bit_length())
 
     own_rows = pl.ds(pl.multiple_of((z * 2 + h) * RB, RB), RB)
     sub_at_dest = rem(h + c, 2)
@@ -133,35 +136,45 @@
         rows = pl.ds(pl.multiple_of((z * 2 + rem(h + sub, 2)) * RB, RB), RB)
         remote(wbr.at[0, k], wg.at[k, :, rows, :], ex_s.at[0], ex_r.at[k * 2 + sub], sibling).wait_recv()
 
-    def ag(k, j, step, sub):
-        b = rem(z + NZ - step, NZ) if j == 0 else rem(z + step, NZ)
+    FAR = NZ // 2
+
+    def hops(j, way):
+        return FAR if j == way else NZ - 1 - FAR
+
+    def slot(k, j, way, step, sub):
+        return (((k * 2 + j) * 2 + way) * FAR + step) * 2 + sub
+
+    def ag_copy(k, j, way, step, sub, back):
+        b = rem(z + 2 * NZ - step - back, NZ) if way == 0 else rem(z + step + back, NZ)
         rows = pl.ds(pl.multiple_of((b * 2 + rem(h + sub, 2)) * RB, RB), RB)
-        n = ((k * 2 + j) * (NZ - 1) + step) * 2 + sub
-        return remote(wg.at[k, j, rows, :], wg.at[k, j, rows, :], ag_s.at[n], ag_r.at[n], zdev[j])
-
-    def ag_wait(k, j, step, sub):
-        b = rem(z + 2 * NZ - 1 - step, NZ) if j == 0 else rem(z + 1 + step, NZ)
-        rows = pl.ds(pl.multiple_of((b * 2 + rem(h + sub, 2)) * RB, RB), RB)
-        n = ((k * 2 + j) * (NZ - 1) + step) * 2 + sub
-        remote(wg.at[k, j, rows, :], wg.at[k, j, rows, :], ag_s.at[n], ag_r.at[n], zdev[j]).wait_recv()
-
-    def ag_relay(k, step, last=None):
+        n = slot(k, j, way, step, sub)
+        return remote(wg.at[k, j, rows, :], wg.at[k, j, rows, :], ag_s.at[n], ag_r.at[n], zdev[way])
+
+    def ag(k, j, way, step, sub):
+        return ag_copy(k, j, way, step, sub, 0)
+
+    def ag_first(k, sub):
+        for way in range(2):
+            for j in range(2):
+                ag(k, j, way, 0, sub).start()
+
+    def ag_relay(k, step):
         for sub in range(2):
-            for j in range(2):
-                ag_wait(k, j, step, sub)
-                if last is None:
-                    @pl.when(step < NZ - 2)
+            for way in range(2):
+                for j in range(2):
+                    @pl.when(step < hops(j, way))
                     def _():
-                        ag(k, j, step + 1, sub).start()
-                elif not last:
-                    ag(k, j, step + 1, sub).start()
+                        ag_copy(k, j, way, step, sub, 1).wait_recv()
+
+                    @pl.when(step < hops(j, way) - 1)
+                    def _():
+                        ag(k, j, way, step + 1, sub).start()
 
     for k in range(CHUNKS):
         @pl.when(c != h)
         def _():
             exchange_wait(k, 0)
-        for j in range(2):
-            ag(k, j, 0, 0).start()
+        ag_first(k, 0)
 
     load_pool.wait()
     TB = min(LANES, TOK)
@@ -185,8 +198,7 @@
 
     for k in range(CHUNKS):
         exchange_wait(k, 1)
-        for j in range(2):
-            ag(k, j, 0, 1).start()
+        ag_first(k, 1)
 
     def slice_out(d):
         q = rem(p + d, NP)
@@ -243,13 +255,19 @@
         def _(d):
             slice_wait(d)
 
+        d1[...] = jnp.zeros_like(d1)
+
         @pl.loop(0, NP)
         def _(i):
             own = wa[i].astype(F32)
-            for j in range(NP):
+            for ahead in range(1, NP // 2 + 1):
+                j = rem(i + ahead, NP)
                 off = own - wa[j].astype(F32)
-                d1[i, j:j + 1, :] = jnp.sum(off * off, axis=0, keepdims=True)
-
+                squares = jnp.sum(off * off, axis=0, keepdims=True)
+                d1[i, pl.ds(j, 1), :] = squares
+                d1[j, pl.ds(i, 1), :] = squares
+
+    def send_distances():
         flat = d1[...].reshape(NP * NP, LANES)
         spread = jnp.dot(flat, jnp.ones((LANES, LANES), F32), precision=HIGHEST, preferred_element_type=F32)
         for i in range(NP):
@@ -261,50 +279,42 @@
         def _(d):
             part_out(d).start()
 
-    pair_out = remote(dpair.at[0], dpair.at[1], dh_s, dh_r, across)
-
-    def pair_distances():
-        dpart[p] = dmine[...]
-
-        @pl.loop(1, NP)
-        def _(d):
-            part_wait(d)
-
-        dpair[0] = jnp.sum(dpart[...], axis=0)
-        pair_out.start()
-
-    def ring_out(step):
-        b = rem(z + NZ - step, NZ)
-        return remote(dring.at[b], dring.at[b], dz_s.at[step], dz_r.at[step], zdev[0])
-
-    def ring_wait(step):
-        b = rem(z + 2 * NZ - 1 - step, NZ)
-        remote(dring.at[b], dring.at[b], dz_s.at[step], dz_r.at[step], zdev[0]).wait_recv()
-
-    def ring_start():
-        pair_out.wait_recv()
-        dring[z] = dpair[0] + dpair[1]
-        ring_out(0).start()
-
-    def ring_relay(step, last=None):
-        ring_wait(step)
-        if last is None:
-            @pl.when(step < NZ - 2)
-            def _():
-                ring_out(step + 1).start()
-        elif not last:
-            ring_out(step + 1).start()
+    BITS = NS.bit_length() - 1
+
+    def pair_out(bit):
+        mask = 1 << bit
+        low = rem(s // mask, 2)
+        return remote(dpair.at[bit, 0], dpair.at[bit, 1], dh_s.at[bit], dh_r.at[bit], (p, s + mask - 2 * mask * low))
+
+    def sum_distances(bit):
+        if bit == 0:
+            dpart[p] = dmine[...]
+
+            @pl.loop(1, NP)
+            def _(d):
+                part_wait(d)
+
+            total = jnp.sum(dpart[...], axis=0)
+        else:
+            pair_out(bit - 1).wait_recv()
+            total = dpair[bit - 1, 0] + dpair[bit - 1, 1]
+        dpair[bit, 0] = total
+        if bit < BITS:
+            pair_out(bit).start()
 
     inverse_band = 1.0 / jnp.full((1, LANES), scale_ref[0], jnp.int32).astype(F32)
     repulse = 2.0 * inverse_band
 
     def kernel_matrix():
-        near = jnp.exp(-jnp.sum(dring[...], axis=0) * inverse_band)
+        near = jnp.exp(-dpair[BITS, 0] * inverse_band)
         for i in range(NP):
             d1[i] = jnp.where(eye, jnp.broadcast_to(near[i:i + 1, :], (NP, LANES)), 0.0)
         flat = d1[...].reshape(NP * NP, LANES)
         spread = jnp.dot(flat, jnp.ones((LANES, LANES), F32), precision=HIGHEST, preferred_element_type=F32)
         krep[...] = spread.reshape(NP, NP, LANES)
+
+    def turn(source, target, hb, at):
+        target[:, pl.ds(pl.multiple_of(hb * TOK + at, HT), HT)] = source[hb, pl.ds(at, HT), :].T
 
     def hidden(k, blk, flip):
         hb = rem(h + blk // 2, 2)
@@ -318,59 +328,62 @@
         act[k, pl.ds(rows, HT), :] = act_full.astype(BF16)
         upg[k, pl.ds(rows, HT), :] = (back_proj * gelu_slope).astype(BF16)
         if flip:
-            nt[:, pl.ds(rows, HT)] = normed.T
-            ct[:, pl.ds(rows, HT)] = upstream.T
+            @pl.when(blk >= 2)
+            def _():
+                turn(na, nt, hb, at)
+                turn(ca, ct, hb, at)
 
     def gradient(k, j, b):
         lhs = (nt if j == 0 else ct)[pl.ds(pl.multiple_of(b * 2 * RB, 2 * RB), 2 * RB), :]
         return jnp.dot(lhs, (upg if j == 0 else act)[k], preferred_element_type=F32)
 
-    def rs(k, j, step, sub):
-        n = ((k * 2 + j) * (NZ - 1) + step) * 2 + sub
-        return remote(rss.at[n], rsr.at[n], rs_s.at[n], rs_r.at[n], zdev[j])
+    def rs(k, j, way, step, sub):
+        n = slot(k, j, way, step, sub)
+        return remote(rss.at[n], rsr.at[n], rs_s.at[n], rs_r.at[n], zdev[way])
+
+    def rs_part(k, j, way, step, first):
+        left = hops(j, way) - step
+        part = gradient(k, j, rem(z + left, NZ) if way == 0 else rem(z + NZ - left, NZ))
+        for sub in range(2):
+            total = part[sub * RB:(sub + 1) * RB, :]
+            n = slot(k, j, way, step, sub)
+            if not first:
+                rs(k, j, way, step - 1, sub).wait_recv()
+                total = total + rsr[n - 2].astype(F32)
+            rss[n] = total.astype(BF16)
+            rs(k, j, way, step, sub).start()
 
     def rs_step(k, step, first=False):
-        parts = [
-            gradient(k, 0, rem(z + 2 * NZ - 1 - step, NZ)),
-            gradient(k, 1, rem(z + 1 + step, NZ)),
-        ]
+        for way in range(2):
+            for j in range(2):
+                @pl.when(step < hops(j, way))
+                def _():
+                    rs_part(k, j, way, step, first)
+
+    grad_scale = 1.0 / (TOK * NZ * 2 * D)
+
+    def score_out(k, o, sub):
+        return remote(sc.at[k, sub, o], sa.at[k, role], sa_s.at[k * NP + o * 2 + sub], sa_r.at[k * NP + role],
+                      (o * 2 + c, z * 2 + sub))
+
+    def rs_final(k):
+        parts = [gradient(k, j, z) for j in range(2)]
         for sub in range(2):
             for j in range(2):
                 total = parts[j][sub * RB:(sub + 1) * RB, :]
-                n = ((k * 2 + j) * (NZ - 1) + step) * 2 + sub
-                if not first:
-                    rs(k, j, step - 1, sub).wait_recv()
-                    total = total + rsr[n - 2].astype(F32)
-                rss[n] = total.astype(BF16)
-                rs(k, j, step, sub).start()
-
-    grad_scale = 1.0 / (TOK * NZ * 2 * D)
-
-    def rs_final(k):
-        for j in range(2):
-            part = gradient(k, j, z)
-            factor = (D if j == 0 else FF) ** (-0.5) * grad_scale
-            for sub in range(2):
-                n = ((k * 2 + j) * (NZ - 1) + NZ - 2) * 2 + sub
-                rs(k, j, NZ - 2, sub).wait_recv()
-                total = part[sub * RB:(sub + 1) * RB, :] + rsr[n].astype(F32)
+                for way in range(2):
+                    rs(k, j, way, hops(j, way) - 1, sub).wait_recv()
+                    total = total + rsr[slot(k, j, way, hops(j, way) - 1, sub)].astype(F32)
+                factor = (D if j == 0 else FF) ** (-0.5) * grad_scale
                 score = (total * -factor).astype(BF16)
                 for tile in range(TC):
                     sc[k, sub, tile * 2 + j] = score[:, tile * LANES:(tile + 1) * LANES]
-
-    def score_out(k, d):
-        r = rem(role + d, NP)
-        return remote(sc.at[k, rem(r, 2), r // 2], sa.at[k, role], sa_s.at[k * NP + d], sa_r.at[k * NP + d],
-                      (r // 2 * 2 + c, z * 2 + rem(r, 2)))
-
-    def score_wait(k, d):
-        r = rem(role + NP - d, NP)
-        remote(sc.at[k, 0, 0], sa.at[k, r], sa_s.at[k * NP + d], sa_r.at[k * NP + d], sibling).wait_recv()
-
-    def send_scores(k):
-        @pl.loop(1, NP)
-        def _(d):
-            score_out(k, d).start()
+                for n in range(TC):
+                    o = rem(xy // 2 + n, TC) * 2 + j
+
+                    @pl.when(o * 2 + sub != role)
+                    def _():
+                        score_out(k, o, sub).start()
 
         sa[k, role] = sc[k, h, xy]
 
@@ -385,15 +398,16 @@
     params_total = 2 * D * FF
 
     def move(k):
-        @pl.loop(1, NP)
+        for q in range(NP):
+            @pl.when(q != role)
+            def _():
+                remote(sc.at[k, 0, 0], sa.at[k, q], sa_s.at[0], sa_r.at[k * NP + q], sibling).wait_recv()
+
+            fld[q] = sa[k, q].astype(F32) - repulse * wa[q, k * RB:(k + 1) * RB, :].astype(F32)
+
+        @pl.loop(1, NP + 1)
         def _(d):
-            score_wait(k, d)
-
-        for q in range(NP):
-            fld[q] = sa[k, q].astype(F32) - repulse * wa[q, k * RB:(k + 1) * RB, :].astype(F32)
-
-        @pl.loop(0, NP)
-        def _(i):
+            i = rem(p + d, NP)
             weighted = krep[i, 0:1, :] * fld[0]
             for j in range(1, NP):
                 weighted = weighted + krep[i, j:j + 1, :] * fld[j]
@@ -401,9 +415,9 @@
             own_w = wa[i, k * RB:(k + 1) * RB, :].astype(F32)
             tr[k, i] = (params_total / NP * (weighted + repulse * kernel_total * own_w)).astype(BF16)
 
-        @pl.loop(1, NP)
-        def _(d):
-            transport_out(k, d).start()
+            @pl.when(d < NP)
+            def _():
+                transport_out(k, d).start()
 
         ta[k, p] = tr[k, p]
 
@@ -412,20 +426,13 @@
         def _(d):
             transport_wait(k, d)
 
-        for q in range(NP):
-            o, half = q // 2, q % 2
-            t = (half * CHUNKS + k) * TC + o // 2
-            out_ref[pl.ds(2 * t + o % 2, RB, stride=2 * NT), :] = ta[k, q].astype(F32)
-
-    LAST = NZ - 2
-    for step in range(NZ - 1):
-        ag_relay(0, step, step == LAST)
-        if step == min(3, LAST):
-            share_segments()
-        if step == min(4, LAST):
-            partial_distances()
-    pair_distances()
-    pass_cotangent()
+        out_ref[k] = ta[k]
+
+    ag_relay(0, 0)
+    for half in range(2):
+        turn(na, nt, h, half * HT)
+    ag_relay(0, 1)
+    share_segments()
 
     @pl.when(c == h)
     def _():
@@ -435,8 +442,14 @@
     def _():
         remote(cot_hbm, ca.at[h], cot_s.at[0], cot_r.at[0], sibling).wait_recv()
 
-    ring_start()
-    EARLY = min(4, NZ - 1)
+    for half in range(2):
+        turn(ca, ct, h, half * HT)
+    ag_relay(0, 2)
+    partial_distances()
+    ag_relay(1, 0)
+    send_distances()
+    ag_relay(0, 3)
+    pass_cotangent()
 
     @pl.loop(0, 4)
     def _(blk):
@@ -450,38 +463,39 @@
 
         hidden(0, blk, True)
 
-        @pl.when(blk < EARLY)
+        @pl.when(blk < 3)
         def _():
-            ag_relay(1, blk)
-            ring_relay(blk)
+            ag_relay(1, blk + 1)
+
+        for bit in range(2):
+            @pl.when(blk == bit + 2)
+            def _():
+                sum_distances(bit)
 
     rs_step(0, 0, True)
-    for step in range(EARLY, NZ - 1):
-        ag_relay(1, step, step == LAST)
-        ring_relay(step, step == LAST)
-        rs_step(0, step - EARLY + 1)
-    kernel_matrix()
-    DONE = NZ - 1 - EARLY
 
     @pl.loop(0, 4)
     def _(blk):
         hidden(1, blk, False)
 
-        @pl.when(DONE + 1 + blk <= LAST)
+        @pl.when(blk < 3)
         def _():
-            rs_step(0, DONE + 1 + blk)
+            rs_step(0, blk + 1)
+
+        for bit in range(2, BITS + 1):
+            @pl.when(blk == bit - 2)
+            def _():
+                sum_distances(bit)
 
     rs_step(1, 0, True)
     rs_final(0)
-    send_scores(0)
-    for step in range(1, NZ - 1):
-        rs_step(1, step)
-        if step == min(3, LAST):
-            move(0)
-        if step == min(6, LAST):
-            collect(0)
+    kernel_matrix()
+    rs_step(1, 1)
+    rs_step(1, 2)
+    move(0)
+    rs_step(1, 3)
+    collect(0)
     rs_final(1)
-    send_scores(1)
     move(1)
     collect(1)
 
@@ -501,7 +515,8 @@
 
     nseg.wait_send()
     cot_pass.wait_send()
-    pair_out.wait_send()
+    for bit in range(BITS):
+        pair_out(bit).wait_send()
 
     @pl.loop(1, G)
     def _(d):
@@ -512,17 +527,23 @@
         slice_out(d).wait_send()
         part_out(d).wait_send()
         for k in range(CHUNKS):
-            score_out(k, d).wait_send()
             transport_out(k, d).wait_send()
 
-    @pl.loop(0, NZ - 1)
-    def _(step):
-        ring_out(step).wait_send()
-        for k in range(CHUNKS):
-            for j in range(2):
-                for sub in range(2):
-                    ag(k, j, step, sub).wait_send()
-                    rs(k, j, step, sub).wait_send()
+    for k in range(CHUNKS):
+        for o in range(NXY):
+            for sub in range(2):
+                @pl.when(o * 2 + sub != role)
+                def _():
+                    score_out(k, o, sub).wait_send()
+
+    for k in range(CHUNKS):
+        for j in range(2):
+            for way in range(2):
+                @pl.loop(0, hops(j, way))
+                def _(step):
+                    for sub in range(2):
+                        ag(k, j, way, step, sub).wait_send()
+                        rs(k, j, way, step, sub).wait_send()
 
 
 def stein_transport(NP, NS, kernel_scale, batch_index, flat_w, pool, cotangent):
@@ -536,7 +557,7 @@
     CH = TC * LANES
     assert TC * 2 == NXY
     dma = pltpu.SemaphoreType.DMA
-    ring = CHUNKS * 2 * (NZ - 1) * 2
+    ring = CHUNKS * 2 * 2 * (NZ // 2) * 2
     scratch = [
         pltpu.VMEM(flat_w.shape, F32),
         pltpu.VMEM((POOL, D), BF16),
@@ -560,8 +581,7 @@
         pltpu.VMEM((NP, NP, LANES), F32),
         pltpu.VMEM((NP, LANES), F32),
         pltpu.VMEM((NP, NP, LANES), F32),
-        pltpu.VMEM((2, NP, LANES), F32),
-        pltpu.VMEM((NZ, NP, LANES), F32),
+        pltpu.VMEM((NS.bit_length(), 2, NP, LANES), F32),
         pltpu.VMEM((NP, NP, LANES), F32),
         dma((3,)),
         dma((2 * CHUNKS,)), dma((2 * CHUNKS,)),
@@ -569,25 +589,56 @@
         dma(()), dma(()), dma((G,)), dma((G,)),
         dma((NP,)), dma((NP,)),
         dma((ring,)), dma((ring,)), dma((ring,)), dma((ring,)),
-        dma((NP,)), dma((NP,)), dma(()), dma(()),
-        dma((NZ - 1,)), dma((NZ - 1,)),
+        dma((NP,)), dma((NP,)), dma((NS.bit_length(),)), dma((NS.bit_length(),)),
         dma((CHUNKS * NP,)), dma((CHUNKS * NP,)), dma((CHUNKS * NP,)), dma((CHUNKS * NP,)),
     ]
     anywhere = pl.BlockSpec(memory_space=pl.ANY)
     vmem = pl.BlockSpec(memory_space=pltpu.VMEM)
     return pl.pallas_call(
-        functools.partial(stein_kernel, (NP, NZ, RB, TOK, D, FF, POOL)),
-        out_shape=jax.ShapeDtypeStruct(flat_w.shape, F32),
+        functools.partial(stein_kernel, (NP, NS, RB, TOK, D, FF, POOL)),
+        out_shape=jax.ShapeDtypeStruct((CHUNKS, NP, RB, LANES), BF16),
         in_specs=[pl.BlockSpec(memory_space=pltpu.SMEM), vmem, anywhere, anywhere, anywhere],
         out_specs=vmem,
         scratch_shapes=scratch,
         compiler_params=pltpu.CompilerParams(
-            collective_id=0, has_side_effects=True, vmem_limit_bytes=60 * 1024 * 1024
+            collective_id=0, has_side_effects=True, vmem_limit_bytes=62 * 1024 * 1024
         ),
         name="stein",
     )(kernel_scale, batch_index.reshape(1, TOK), flat_w, pool, cotangent)
 
 
+def adam_kernel(NT, moved_ref, w_ref, m_ref, v_ref, new_w, new_m, new_v, transport_ref):
+    NP, rows = moved_ref.shape[1:3]
+    TC = NT // 2 // CHUNKS
+    for k in range(CHUNKS):
+        for q in range(NP):
+            o, half = q // 2, q % 2
+            t = (half * CHUNKS + k) * TC + o // 2
+            transport_ref[pl.ds(2 * t + o % 2, rows, stride=2 * NT), :] = moved_ref[k, q].astype(F32)
+    transport = transport_ref[...]
+    new_first = 0.9 * m_ref[...] - 0.1 * transport
+    new_second = 0.999 * v_ref[...] + 0.001 * transport * transport
+    new_m[...] = new_first
+    new_v[...] = new_second
+    new_w[...] = w_ref[...] - 0.01 * new_first / (jnp.sqrt(new_second) + 1e-08)
+
+
+def adam(moved, flat_w, flat_m, flat_v):
+    chunks, NP, RB, lanes = moved.shape
+    steps = RB // 16
+    size = flat_w.shape[0] // steps
+    block = pl.BlockSpec((size, lanes), lambda i: (i, 0))
+    shape = jax.ShapeDtypeStruct(flat_w.shape, F32)
+    return pl.pallas_call(
+        functools.partial(adam_kernel, flat_w.shape[0] // RB // 2),
+        out_shape=(shape,) * 4,
+        grid=(steps,),
+        in_specs=[pl.BlockSpec((chunks, NP, 16, lanes), lambda i: (0, 0, i, 0)), block, block, block],
+        out_specs=(block,) * 4,
+        name="adam",
+    )(moved, flat_w, flat_m, flat_v)
+
+
 def local(NP, NS, pool, batch_index, kernel_scale, cotangent, weights, first_moment, second_moment):
     rows, pair, hidden_units = weights.shape[1:]
 
@@ -599,11 +650,9 @@
         return a.reshape(1, rows, pair, hidden_units)
 
     flat_w = flatten(weights[0])
-    transport = stein_transport(NP, NS, kernel_scale, batch_index, flat_w, pool, cotangent[0])
-    new_first = 0.9 * flatten(first_moment[0]) - 0.1 * transport
-    new_second = 0.999 * flatten(second_moment[0]) + 0.001 * transport * transport
-    new_weights = flat_w - 0.01 * new_first / (jnp.sqrt(new_second) + 1e-08)
-    return tuple(unflatten(a) for a in (new_weights, new_first, new_second, transport))
+    moved = stein_transport(NP, NS, kernel_scale, batch_index, flat_w, pool, cotangent[0])
+    outs = adam(moved, flat_w, flatten(first_moment[0]), flatten(second_moment[0]))
+    return tuple(unflatten(a) for a in outs)
 
 
 def solution(mesh):

time: 152 us -> 131 us (0.86)
  Pallas kernels: 145 us -> 129 us
  other arithmetic: 3.1 us -> 0 us
  local copies, waits for them, and re-layouts: 1.6 us -> 0 us
    pallas_call x1 -> x2, Pallas kernels: 145 us -> 129 us  [the longest x1 124 us: stein_transport(): pl.pallas_call(functools.partial(stein_kernel, (NP, NS, RB, TOK, D, FF, P...]
    sub x1 -> x0, other arithmetic: 1.92 us -> none  [local(): new_weights = flat_w - 0.01 * new_first / (jnp.sqrt(new_second) + 1e-08)]
    unnamed x9 -> x0, local copies, waits for them, and re-layouts: 1.6 us -> none
where the time goes in v2:
time: 131 us
  Pallas kernels  129 us (98%)
    pallas_call x1, Pallas kernels, stein_transport(): pl.pallas_call(functools.partial(stein_kernel, (NP, NS, RB, TOK, D, FF, P...  124 us
    pallas_call x1, Pallas kernels, adam(): pl.pallas_call(functools.partial(adam_kernel, flat_w.shape[0] // RB // 2)...  5.13 us

profile of v2, /device:TPU:1, one launch (start us, length us, event | category | flops | bytes accessed | tf_op | source)
XLA Modules:
  0.0 130.7 jit_solution(9773883829852527584)
XLA Ops:
  1.3 124.2 %stein.1.moved_ref = bf16[2,16,64,128]{3,2,1,0:T(8,128)(2,1)} custom-call(s32[1]{0:T(128)S(6)} %copy.18.scale_ref, s32[1,512]{1,0:T(1,128)} %bitcast.42, f32[2048,128]{1,0:T(8,128)} %bitcast.37, bf16[1024,1024]{1,0:T(8,128)(2,1)} %pool_hbm.1, bf16[512,1024]{1,0:T(8,128)(2,1)} %bitcast.41), custom_call_target="tpu_custom_call" | custom-call | tf_op jit(solution)/shard_map/stein/pallas_call | solution.py:597
  125.5 5.1 %adam.1 = (f32[2048,128]{1,0:T(8,128)}, f32[2048,128]{1,0:T(8,128)}, f32[2048,128]{1,0:T(8,128)}, f32[2048,128]{1,0:T(8,128)}) custom-call(bf16[2,16,64,128]{3,2,1,0:T(8,128)(2,1)} %stein.1.moved_ref, f32[2048,128]{1,0:T(8,128)} %bitcast.38, f32[2048,128]{1,0:T(8,128)} %bitcast.39, f32[2048,128]{1,0:T(8,128)} %bitcast.40), custom_call_target="tpu_custom_call" | custom-call | tf_op jit(solution)/shard_map/adam/pallas_call | solution.py:632

commit v3 on v2

--- a/solution.py
+++ b/solution.py
@@ -208,11 +208,12 @@
         q = rem(p + NP - d, NP)
         remote(wba.at[q], wa.at[q], wa_s.at[d], wa_r.at[d], (q, s)).wait_recv()
 
-    @pl.loop(1, NP)
-    def _(d):
-        slice_out(d).start()
-
-    wa[p] = wba[p]
+    def send_slices():
+        @pl.loop(1, NP)
+        def _(d):
+            slice_out(d).start()
+
+        wa[p] = wba[p]
 
     got_seg = na.at[1 - h, pl.ds(pl.multiple_of(seg * SEG, SEG), SEG)]
 
@@ -428,11 +429,73 @@
 
         out_ref[k] = ta[k]
 
+    def drain_gather():
+        @pl.when(c == h)
+        def _():
+            for k in range(CHUNKS):
+                exchange(k, 1 - c, sibling).wait_send()
+            cot_full.wait_send()
+
+        @pl.when(c != h)
+        def _():
+            for k in range(CHUNKS):
+                for half in range(2):
+                    exchange(k, half, (xy * 2 + half, z * 2 + 1 - h)).wait_send()
+            for half in range(2):
+                cot_half(half).wait_send()
+
+        nseg.wait_send()
+        cot_pass.wait_send()
+
+        @pl.loop(1, G)
+        def _(d):
+            seg_out(d).wait_send()
+
+        @pl.loop(1, NP)
+        def _(d):
+            slice_out(d).wait_send()
+            part_out(d).wait_send()
+
+        for k in range(CHUNKS):
+            for j in range(2):
+                for way in range(2):
+                    @pl.loop(0, hops(j, way))
+                    def _(step):
+                        for sub in range(2):
+                            ag(k, j, way, step, sub).wait_send()
+
+    def drain_ring():
+        for bit in range(BITS):
+            pair_out(bit).wait_send()
+
+        for k in range(CHUNKS):
+            for j in range(2):
+                for way in range(2):
+                    @pl.loop(0, hops(j, way))
+                    def _(step):
+                        for sub in range(2):
+                            rs(k, j, way, step, sub).wait_send()
+
+    def drain_scores():
+        for k in range(CHUNKS):
+            for o in range(NXY):
+                for sub in range(2):
+                    @pl.when(o * 2 + sub != role)
+                    def _():
+                        score_out(k, o, sub).wait_send()
+
+    def drain_transport():
+        @pl.loop(1, NP)
+        def _(d):
+            for k in range(CHUNKS):
+                transport_out(k, d).wait_send()
+
     ag_relay(0, 0)
     for half in range(2):
         turn(na, nt, h, half * HT)
     ag_relay(0, 1)
     share_segments()
+    send_slices()
 
     @pl.when(c == h)
     def _():
@@ -445,9 +508,7 @@
     for half in range(2):
         turn(ca, ct, h, half * HT)
     ag_relay(0, 2)
-    partial_distances()
     ag_relay(1, 0)
-    send_distances()
     ag_relay(0, 3)
     pass_cotangent()
 
@@ -463,87 +524,50 @@
 
         hidden(0, blk, True)
 
+        @pl.when(blk < 2)
+        def _():
+            ag_relay(1, blk + 1)
+
+    rs_step(0, 0, True)
+    ag_relay(1, 3)
+
+    @pl.loop(0, 4)
+    def _(blk):
+        hidden(1, blk, False)
+
         @pl.when(blk < 3)
         def _():
-            ag_relay(1, blk + 1)
+            rs_step(0, blk + 1)
+
+        @pl.when(blk == 0)
+        def _():
+            partial_distances()
+            send_distances()
 
         for bit in range(2):
             @pl.when(blk == bit + 2)
             def _():
                 sum_distances(bit)
 
-    rs_step(0, 0, True)
-
-    @pl.loop(0, 4)
-    def _(blk):
-        hidden(1, blk, False)
-
-        @pl.when(blk < 3)
-        def _():
-            rs_step(0, blk + 1)
-
-        for bit in range(2, BITS + 1):
-            @pl.when(blk == bit - 2)
-            def _():
-                sum_distances(bit)
-
     rs_step(1, 0, True)
     rs_final(0)
+    sum_distances(2)
+    drain_gather()
+    rs_step(1, 1)
+    for bit in range(3, BITS):
+        sum_distances(bit)
+    rs_step(1, 2)
+    sum_distances(BITS)
     kernel_matrix()
-    rs_step(1, 1)
-    rs_step(1, 2)
+    rs_step(1, 3)
     move(0)
-    rs_step(1, 3)
+    drain_ring()
     collect(0)
     rs_final(1)
     move(1)
+    drain_scores()
     collect(1)
-
-    @pl.when(c == h)
-    def _():
-        for k in range(CHUNKS):
-            exchange(k, 1 - c, sibling).wait_send()
-        cot_full.wait_send()
-
-    @pl.when(c != h)
-    def _():
-        for k in range(CHUNKS):
-            for half in range(2):
-                exchange(k, half, (xy * 2 + half, z * 2 + 1 - h)).wait_send()
-        for half in range(2):
-            cot_half(half).wait_send()
-
-    nseg.wait_send()
-    cot_pass.wait_send()
-    for bit in range(BITS):
-        pair_out(bit).wait_send()
-
-    @pl.loop(1, G)
-    def _(d):
-        seg_out(d).wait_send()
-
-    @pl.loop(1, NP)
-    def _(d):
-        slice_out(d).wait_send()
-        part_out(d).wait_send()
-        for k in range(CHUNKS):
-            transport_out(k, d).wait_send()
-
-    for k in range(CHUNKS):
-        for o in range(NXY):
-            for sub in range(2):
-                @pl.when(o * 2 + sub != role)
-                def _():
-                    score_out(k, o, sub).wait_send()
-
-    for k in range(CHUNKS):
-        for j in range(2):
-            for way in range(2):
-                @pl.loop(0, hops(j, way))
-                def _(step):
-                    for sub in range(2):
-                        ag(k, j, way, step, sub).wait_send()
-                        rs(k, j, way, step, sub).wait_send()
+    drain_transport()
 
 
 def stein_transport(NP, NS, kernel_scale, batch_index, flat_w, pool, cotangent):
@@ -592,7 +616,7 @@
         dma((NP,)), dma((NP,)), dma((NS.bit_length(),)), dma((NS.bit_length(),)),
         dma((CHUNKS * NP,)), dma((CHUNKS * NP,)), dma((CHUNKS * NP,)), dma((CHUNKS * NP,)),
     ]
-    anywhere = pl.BlockSpec(memory_space=pl.ANY)
+    anywhere = pl.BlockSpec(memory_space=pltpu.HBM)
     vmem = pl.BlockSpec(memory_space=pltpu.VMEM)
     return pl.pallas_call(
         functools.partial(stein_kernel, (NP, NS, RB, TOK, D, FF, POOL)),
@@ -601,40 +625,51 @@
         out_specs=vmem,
         scratch_shapes=scratch,
         compiler_params=pltpu.CompilerParams(
-            collective_id=0, has_side_effects=True, vmem_limit_bytes=62 * 1024 * 1024
+            collective_id=0, has_side_effects=True, vmem_limit_bytes=56 * 1024 * 1024
         ),
         name="stein",
     )(kernel_scale, batch_index.reshape(1, TOK), flat_w, pool, cotangent)
 
 
-def adam_kernel(NT, moved_ref, w_ref, m_ref, v_ref, new_w, new_m, new_v, transport_ref):
+def adam_kernel(NT, parts, moved_ref, w_ref, m_ref, v_ref, new_w, new_m, new_v, transport_ref, out, sems):
     NP, rows = moved_ref.shape[1:3]
     TC = NT // 2 // CHUNKS
-    for k in range(CHUNKS):
-        for q in range(NP):
-            o, half = q // 2, q % 2
-            t = (half * CHUNKS + k) * TC + o // 2
-            transport_ref[pl.ds(2 * t + o % 2, rows, stride=2 * NT), :] = moved_ref[k, q].astype(F32)
-    transport = transport_ref[...]
-    new_first = 0.9 * m_ref[...] - 0.1 * transport
-    new_second = 0.999 * v_ref[...] + 0.001 * transport * transport
-    new_m[...] = new_first
-    new_v[...] = new_second
-    new_w[...] = w_ref[...] - 0.01 * new_first / (jnp.sqrt(new_second) + 1e-08)
+    part_rows = rows // parts
+    size = part_rows * 2 * NT
+    copies = []
+    for part in range(parts):
+        span = pl.ds(part * size, size)
+        for k in range(CHUNKS):
+            for q in range(NP):
+                o, half = q // 2, q % 2
+                t = (half * CHUNKS + k) * TC + o // 2
+                piece = moved_ref[k, q, part * part_rows:(part + 1) * part_rows, :].astype(F32)
+                out[0, pl.ds(part * size + 2 * t + o % 2, part_rows, stride=2 * NT), :] = piece
+        transport = out[0, span, :]
+        new_first = 0.9 * m_ref[span, :] - 0.1 * transport
+        new_second = 0.999 * v_ref[span, :] + 0.001 * transport * transport
+        out[1, span, :] = new_first
+        out[2, span, :] = new_second
+        out[3, span, :] = w_ref[span, :] - 0.01 * new_first / (jnp.sqrt(new_second) + 1e-08)
+        for n, target in enumerate((transport_ref, new_m, new_v, new_w)):
+            copy = pltpu.make_async_copy(out.at[n, span], target.at[span], sems.at[n, part])
+            copy.start()
+            copies.append(copy)
+    for copy in copies:
+        copy.wait()
 
 
 def adam(moved, flat_w, flat_m, flat_v):
-    chunks, NP, RB, lanes = moved.shape
-    steps = RB // 16
-    size = flat_w.shape[0] // steps
-    block = pl.BlockSpec((size, lanes), lambda i: (i, 0))
+    RB, lanes = moved.shape[2:]
+    parts = max(RB // 16, 1)
     shape = jax.ShapeDtypeStruct(flat_w.shape, F32)
     return pl.pallas_call(
-        functools.partial(adam_kernel, flat_w.shape[0] // RB // 2),
+        functools.partial(adam_kernel, flat_w.shape[0] // RB // 2, parts),
         out_shape=(shape,) * 4,
-        grid=(steps,),
-        in_specs=[pl.BlockSpec((chunks, NP, 16, lanes), lambda i: (0, 0, i, 0)), block, block, block],
-        out_specs=(block,) * 4,
+        in_specs=[pl.BlockSpec(memory_space=pltpu.VMEM)] * 4,
+        out_specs=(pl.BlockSpec(memory_space=pltpu.HBM),) * 4,
+        scratch_shapes=[pltpu.VMEM((4,) + flat_w.shape, F32), pltpu.SemaphoreType.DMA((4, parts))],
+        compiler_params=pltpu.CompilerParams(vmem_limit_bytes=16 * 1024 * 1024),
         name="adam",
     )(moved, flat_w, flat_m, flat_v)
 

time: 131 us -> 128 us (0.977)
  Pallas kernels: 129 us -> 125 us
    pallas_call x1, Pallas kernels: 5.13 us -> 2.92 us  [adam(): pl.pallas_call(functools.partial(adam_kernel, flat_w.shape[0] // RB // 2,...]
    pallas_call x1, Pallas kernels: 124 us -> 122 us  [stein_transport(): pl.pallas_call(functools.partial(stein_kernel, (NP, NS, RB, TOK, D, FF, P...]
where the time goes in v3:
time: 128 us; the launch traced here: 127 us
  Pallas kernels  125 us (98%)
  between operations  1.34 us (1%)
    pallas_call x1, Pallas kernels, stein_transport(): pl.pallas_call(functools.partial(stein_kernel, (NP, NS, RB, TOK, D, FF, P...  122 us
    pallas_call x1, Pallas kernels, adam(): pl.pallas_call(functools.partial(adam_kernel, flat_w.shape[0] // RB // 2,...  2.92 us

profile of v3, /device:TPU:1, one launch (start us, length us, event | category | flops | bytes accessed | tf_op | source)
XLA Modules:
  0.0 127.4 jit_solution(10950471814157867036)
XLA Ops:
  1.3 0.0 copy-start
  1.3 0.0 copy-start.2
  1.3 0.0 copy-start.3
  1.3 122.1 %stein.1.moved_ref = bf16[2,16,64,128]{3,2,1,0:T(8,128)(2,1)} custom-call(s32[1]{0:T(128)S(6)} %copy.18.scale_ref, s32[1,512]{1,0:T(1,128)} %bitcast.42, f32[2048,128]{1,0:T(8,128)} %bitcast.37, bf16[1024,1024]{1,0:T(8,128)(2,1)} %pool_hbm.1, bf16[512,1024]{1,0:T(8,128)(2,1)} %bitcast.41), custom_call_target="tpu_custom_call" | custom-call | tf_op jit(solution)/shard_map/stein/pallas_call | solution.py:621
  123.4 0.0 copy-done
  123.5 0.0 copy-done.2
  123.5 0.0 copy-done.3
  123.5 0.0 copy-start.1
  123.5 1.0 copy-done.1
  124.5 2.9 %adam.1 = (f32[2048,128]{1,0:T(8,128)}, f32[2048,128]{1,0:T(8,128)}, f32[2048,128]{1,0:T(8,128)}, f32[2048,128]{1,0:T(8,128)}) custom-call(bf16[2,16,64,128]{3,2,1,0:T(8,128)(2,1)S(1)} %copy-done.1, f32[2048,128]{1,0:T(8,128)S(1)} %bitcast.38, f32[2048,128]{1,0:T(8,128)S(1)} %bitcast.39, f32[2048,128]{1,0:T(8,128)S(1)} %bitcast.40), custom_call_target="tpu_custom_call" | custom-call | tf_op jit(solution)/shard_map/adam/pallas_call | solution.py:666
Async XLA Ops:
  1.3 122.2 %copy-start = (f32[1,64,2,2048]{3,2,1,0:T(2,128)S(1)}, f32[1,64,2,2048]{3,2,1,0:T(2,128)}, u32[]{:S(2)}) copy-start(f32[1,64,2,2048]{3,2,1,0:T(2,128)} %param.11) | copy-start | bytes 3145732
  1.3 122.2 %copy-start.2 = (f32[1,64,2,2048]{3,2,1,0:T(2,128)S(1)}, f32[1,64,2,2048]{3,2,1,0:T(2,128)}, u32[]{:S(2)}) copy-start(f32[1,64,2,2048]{3,2,1,0:T(2,128)} %param.12) | copy-start | bytes 3145732
  1.3 122.2 %copy-start.3 = (f32[1,64,2,2048]{3,2,1,0:T(2,128)S(1)}, f32[1,64,2,2048]{3,2,1,0:T(2,128)}, u32[]{:S(2)}) copy-start(f32[1,64,2,2048]{3,2,1,0:T(2,128)} %param.13) | copy-start | bytes 3145732
  123.5 1.0 copy-start.1

commit v4 on v3

--- a/solution.py
+++ b/solution.py
@@ -34,9 +34,9 @@
 
 def stein_kernel(
     dims,
-    scale_ref, idx_ref, w_hbm, pool_hbm, cot_hbm,
+    scale_hbm, idx_hbm, w_hbm, pool_hbm, cot_hbm,
     out_ref,
-    wf, poolv, wbr, wba, wg, na, ca, nt, ct, act, upg, rss, rsr, sc, sa, wa, fld, tr, ta,
+    scale_ref, idx_ref, wf, poolv, wbr, wba, wg, na, ca, nt, ct, act, upg, rss, rsr, sc, sa, wa, fld, tr, ta,
     d1, dmine, dpart, dpair, krep,
     load_sem, ex_s, ex_r, cot_s, cot_r, cot_fs, cot_fr, nseg_s, nseg_r, nb_s, nb_r,
     wa_s, wa_r, ag_s, ag_r, rs_s, rs_r, dp_s, dp_r, dh_s, dh_r, sa_s, sa_r, ta_s, ta_r,
@@ -68,6 +68,10 @@
     load_w.start()
     load_pool = pltpu.make_async_copy(pool_hbm, poolv, load_sem.at[1])
     load_pool.start()
+    load_idx = pltpu.make_async_copy(idx_hbm, idx_ref, load_sem.at[3])
+    load_idx.start()
+    load_scale = pltpu.make_async_copy(scale_hbm, scale_ref, load_sem.at[4])
+    load_scale.start()
     barrier = pltpu.get_barrier_semaphore()
 
     def greet(device):
@@ -95,7 +99,6 @@
                     t = (half * CHUNKS + k) * TC + tile
                     v = wf[pl.ds(2 * t + j, RB, stride=2 * NT), :].astype(BF16)
                     wbr[half, k, j, :, tile * LANES:(tile + 1) * LANES] = v
-                    wba[(tile * 2 + j) * 2 + half, k * RB:(k + 1) * RB, :] = v
     pl.semaphore_wait(barrier, NP + NXY + NZ.bit_length())
 
     own_rows = pl.ds(pl.multiple_of((z * 2 + h) * RB, RB), RB)
@@ -177,6 +180,8 @@
         ag_first(k, 0)
 
     load_pool.wait()
+    load_idx.wait()
+    load_scale.wait()
     TB = min(LANES, TOK)
 
     @pl.loop(0, TOK // TB)
@@ -209,6 +214,14 @@
         remote(wba.at[q], wa.at[q], wa_s.at[d], wa_r.at[d], (q, s)).wait_recv()
 
     def send_slices():
+        for half in range(2):
+            for k in range(CHUNKS):
+                for tile in range(TC):
+                    for j in range(2):
+                        wba[(tile * 2 + j) * 2 + half, k * RB:(k + 1) * RB, :] = (
+                            wbr[half, k, j, :, tile * LANES:(tile + 1) * LANES]
+                        )
+
         @pl.loop(1, NP)
         def _(d):
             slice_out(d).start()
@@ -495,7 +508,6 @@
         turn(na, nt, h, half * HT)
     ag_relay(0, 1)
     share_segments()
-    send_slices()
 
     @pl.when(c == h)
     def _():
@@ -511,6 +523,7 @@
     ag_relay(1, 0)
     ag_relay(0, 3)
     pass_cotangent()
+    send_slices()
 
     @pl.loop(0, 4)
     def _(blk):
@@ -561,9 +574,9 @@
     kernel_matrix()
     rs_step(1, 3)
     move(0)
+    rs_final(1)
+    collect(0)
     drain_ring()
-    collect(0)
-    rs_final(1)
     move(1)
     drain_scores()
     collect(1)
@@ -583,6 +596,8 @@
     dma = pltpu.SemaphoreType.DMA
     ring = CHUNKS * 2 * 2 * (NZ // 2) * 2
     scratch = [
+        pltpu.SMEM((1,), jnp.int32),
+        pltpu.VMEM((1, TOK), jnp.int32),
         pltpu.VMEM(flat_w.shape, F32),
         pltpu.VMEM((POOL, D), BF16),
         pltpu.VMEM((2, CHUNKS, 2, RB, CH), BF16),
@@ -607,7 +622,7 @@
         pltpu.VMEM((NP, NP, LANES), F32),
         pltpu.VMEM((NS.bit_length(), 2, NP, LANES), F32),
         pltpu.VMEM((NP, NP, LANES), F32),
-        dma((3,)),
+        dma((5,)),
         dma((2 * CHUNKS,)), dma((2 * CHUNKS,)),
         dma((2,)), dma((2,)), dma(()), dma(()),
         dma(()), dma(()), dma((G,)), dma((G,)),
@@ -621,7 +636,7 @@
     return pl.pallas_call(
         functools.partial(stein_kernel, (NP, NS, RB, TOK, D, FF, POOL)),
         out_shape=jax.ShapeDtypeStruct((CHUNKS, NP, RB, LANES), BF16),
-        in_specs=[pl.BlockSpec(memory_space=pltpu.SMEM), vmem, anywhere, anywhere, anywhere],
+        in_specs=[anywhere] * 5,
         out_specs=vmem,
         scratch_shapes=scratch,
         compiler_params=pltpu.CompilerParams(

time: 128 us -> 123 us (0.961)
  Pallas kernels: 125 us -> 120 us
    pallas_call x1, Pallas kernels: 122 us -> 118 us  [stein_transport(): pl.pallas_call(functools.partial(stein_kernel, (NP, NS, RB, TOK, D, FF, P...]
where the time goes in v4:
time: 123 us
  Pallas kernels  120 us (98%)
  between operations  1.34 us (1%)
    pallas_call x1, Pallas kernels, stein_transport(): pl.pallas_call(functools.partial(stein_kernel, (NP, NS, RB, TOK, D, FF, P...  118 us
    pallas_call x1, Pallas kernels, adam(): pl.pallas_call(functools.partial(adam_kernel, flat_w.shape[0] // RB // 2,...  2.92 us

profile of v4, /device:TPU:1, one launch (start us, length us, event | category | flops | bytes accessed | tf_op | source)
XLA Modules:
  0.0 122.8 jit_solution(16129037607330992927)
XLA Ops:
  1.3 0.0 copy-start
  1.3 0.0 copy-start.2
  1.3 0.0 copy-start.3
  1.3 117.5 %stein.1.moved_ref = bf16[2,16,64,128]{3,2,1,0:T(8,128)(2,1)} custom-call(s32[1]{0:T(128)S(6)} %copy.18.scale_hbm, s32[1,512]{1,0:T(1,128)} %bitcast.42, f32[2048,128]{1,0:T(8,128)} %bitcast.37, bf16[1024,1024]{1,0:T(8,128)(2,1)} %pool_hbm.1, bf16[512,1024]{1,0:T(8,128)(2,1)} %bitcast.41), custom_call_target="tpu_custom_call" | custom-call | tf_op jit(solution)/shard_map/stein/pallas_call | solution.py:636
  118.9 0.0 copy-done
  118.9 0.0 copy-done.2
  118.9 0.0 copy-done.3
  118.9 0.0 copy-start.1
  118.9 1.0 copy-done.1
  119.9 2.9 %adam.1 = (f32[2048,128]{1,0:T(8,128)}, f32[2048,128]{1,0:T(8,128)}, f32[2048,128]{1,0:T(8,128)}, f32[2048,128]{1,0:T(8,128)}) custom-call(bf16[2,16,64,128]{3,2,1,0:T(8,128)(2,1)S(1)} %copy-done.1, f32[2048,128]{1,0:T(8,128)S(1)} %bitcast.38, f32[2048,128]{1,0:T(8,128)S(1)} %bitcast.39, f32[2048,128]{1,0:T(8,128)S(1)} %bitcast.40), custom_call_target="tpu_custom_call" | custom-call | tf_op jit(solution)/shard_map/adam/pallas_call | solution.py:681
Async XLA Ops:
  1.3 117.6 %copy-start = (f32[1,64,2,2048]{3,2,1,0:T(2,128)S(1)}, f32[1,64,2,2048]{3,2,1,0:T(2,128)}, u32[]{:S(2)}) copy-start(f32[1,64,2,2048]{3,2,1,0:T(2,128)} %param.11) | copy-start | bytes 3145732
  1.3 117.6 %copy-start.2 = (f32[1,64,2,2048]{3,2,1,0:T(2,128)S(1)}, f32[1,64,2,2048]{3,2,1,0:T(2,128)}, u32[]{:S(2)}) copy-start(f32[1,64,2,2048]{3,2,1,0:T(2,128)} %param.12) | copy-start | bytes 3145732
  1.3 117.6 %copy-start.3 = (f32[1,64,2,2048]{3,2,1,0:T(2,128)S(1)}, f32[1,64,2,2048]{3,2,1,0:T(2,128)}, u32[]{:S(2)}) copy-start(f32[1,64,2,2048]{3,2,1,0:T(2,128)} %param.13) | copy-start | bytes 3145732
  118.9 1.0 copy-start.1

commit v5 on v4

--- a/solution.py
+++ b/solution.py
@@ -92,13 +92,15 @@
         greet((o * 2 + c, z * 2 + 1 - h))
 
     load_w.wait()
-    for half in range(2):
-        for k in range(CHUNKS):
+    def round_weights(k):
+        for half in range(2):
             for tile in range(TC):
                 for j in range(2):
                     t = (half * CHUNKS + k) * TC + tile
                     v = wf[pl.ds(2 * t + j, RB, stride=2 * NT), :].astype(BF16)
                     wbr[half, k, j, :, tile * LANES:(tile + 1) * LANES] = v
+
+    round_weights(0)
     pl.semaphore_wait(barrier, NP + NXY + NZ.bit_length())
 
     own_rows = pl.ds(pl.multiple_of((z * 2 + h) * RB, RB), RB)
@@ -118,20 +120,27 @@
     cot_load = pltpu.make_async_copy(cot_hbm, ca.at[h], load_sem.at[2])
     cot_full = remote(cot_hbm, ca.at[h], cot_s.at[0], cot_r.at[0], sibling)
 
+    for k in range(CHUNKS):
+        if k > 0:
+            round_weights(k)
+
+        @pl.when(c == h)
+        def _():
+            exchange(k, 1 - c, sibling).start()
+            wg[k, :, own_rows, :] = wbr[c, k]
+
+        @pl.when(c != h)
+        def _():
+            for half in range(2):
+                exchange(k, half, (xy * 2 + half, z * 2 + 1 - h)).start()
+
     @pl.when(c == h)
     def _():
-        for k in range(CHUNKS):
-            exchange(k, 1 - c, sibling).start()
-        for k in range(CHUNKS):
-            wg[k, :, own_rows, :] = wbr[c, k]
         cot_load.start()
         cot_full.start()
 
     @pl.when(c != h)
     def _():
-        for k in range(CHUNKS):
-            for half in range(2):
-                exchange(k, half, (xy * 2 + half, z * 2 + 1 - h)).start()
         for half in range(2):
             cot_half(half).start()
 

time: 123 us -> 124 us (level)
  no operation moved by 1% of the time
where the time goes in v5:
time: 124 us
  Pallas kernels  121 us (98%)
  between operations  1.34 us (1%)
    pallas_call x1, Pallas kernels, stein_transport(): pl.pallas_call(functools.partial(stein_kernel, (NP, NS, RB, TOK, D, FF, P...  118 us
    pallas_call x1, Pallas kernels, adam(): pl.pallas_call(functools.partial(adam_kernel, flat_w.shape[0] // RB // 2,...  2.92 us

profile of v5, /device:TPU:1, one launch (start us, length us, event | category | flops | bytes accessed | tf_op | source)
XLA Modules:
  0.0 123.8 jit_solution(15204527713254035992)
XLA Ops:
  1.3 0.0 copy-start
  1.3 0.0 copy-start.2
  1.3 0.0 copy-start.3
  1.3 118.5 %stein.1.moved_ref = bf16[2,16,64,128]{3,2,1,0:T(8,128)(2,1)} custom-call(s32[1]{0:T(128)S(6)} %copy.18.scale_hbm, s32[1,512]{1,0:T(1,128)} %bitcast.42, f32[2048,128]{1,0:T(8,128)} %bitcast.37, bf16[1024,1024]{1,0:T(8,128)(2,1)} %pool_hbm.1, bf16[512,1024]{1,0:T(8,128)(2,1)} %bitcast.41), custom_call_target="tpu_custom_call" | custom-call | tf_op jit(solution)/shard_map/stein/pallas_call | solution.py:645
  119.8 0.0 copy-done
  119.8 0.0 copy-done.2
  119.8 0.0 copy-done.3
  119.8 0.0 copy-start.1
  119.9 1.0 copy-done.1
  120.9 2.9 %adam.1 = (f32[2048,128]{1,0:T(8,128)}, f32[2048,128]{1,0:T(8,128)}, f32[2048,128]{1,0:T(8,128)}, f32[2048,128]{1,0:T(8,128)}) custom-call(bf16[2,16,64,128]{3,2,1,0:T(8,128)(2,1)S(1)} %copy-done.1, f32[2048,128]{1,0:T(8,128)S(1)} %bitcast.38, f32[2048,128]{1,0:T(8,128)S(1)} %bitcast.39, f32[2048,128]{1,0:T(8,128)S(1)} %bitcast.40), custom_call_target="tpu_custom_call" | custom-call | tf_op jit(solution)/shard_map/adam/pallas_call | solution.py:690
Async XLA Ops:
  1.3 118.5 %copy-start = (f32[1,64,2,2048]{3,2,1,0:T(2,128)S(1)}, f32[1,64,2,2048]{3,2,1,0:T(2,128)}, u32[]{:S(2)}) copy-start(f32[1,64,2,2048]{3,2,1,0:T(2,128)} %param.11) | copy-start | bytes 3145732
  1.3 118.5 %copy-start.2 = (f32[1,64,2,2048]{3,2,1,0:T(2,128)S(1)}, f32[1,64,2,2048]{3,2,1,0:T(2,128)}, u32[]{:S(2)}) copy-start(f32[1,64,2,2048]{3,2,1,0:T(2,128)} %param.12) | copy-start | bytes 3145732
  1.3 118.5 %copy-start.3 = (f32[1,64,2,2048]{3,2,1,0:T(2,128)S(1)}, f32[1,64,2,2048]{3,2,1,0:T(2,128)}, u32[]{:S(2)}) copy-start(f32[1,64,2,2048]{3,2,1,0:T(2,128)} %param.13) | copy-start | bytes 3145732
  119.8 1.0 copy-start.1
